TPU v7x, 32 devices: a whole 2x2x4 slice. The times are simulated.
32 devices in a mesh: seq: 4 (over y, x), exp: 8 (over z, core).
Axes of the slice: x: 2, y: 2, z: 4, core: 2. Of those that a mesh axis runs over, the one named last changes fastest.
Arguments:
- tokens: bfloat16 [8, 1024, 1024], P('exp', 'seq'), may hold values from -6 to 6
- lengths: int32 [8, 3], P('exp'), may hold values from 32 to 960, as said below
- expert_ids: int32 [8, 1024, 1], P('exp', 'seq'), may hold values from 0 to 7; in each aligned block of 256 rows (0 to 255, 256 to 511, ..., all dimensions but the last counted through in order) at most 64 rows name the same one
- ln1_gain: bfloat16 [1024], replicated, may hold values from 0.5 to 1.5
- ln1_bias: bfloat16 [1024], replicated, may hold values from -1.25 to 1.25
- w_query: bfloat16 [1024, 1024], replicated, may hold values from -0.25 to 0.25
- b_query: bfloat16 [1024], replicated, may hold values from -1.25 to 1.25
- w_key: bfloat16 [1024, 1024], replicated, may hold values from -0.1875 to 0.1875
- w_value: bfloat16 [1024, 1024], replicated, may hold values from -0.1875 to 0.1875
- b_value: bfloat16 [1024], replicated, may hold values from -1.25 to 1.25
- w_out: bfloat16 [1024, 1024], replicated, may hold values from -1 to 1
- b_out: bfloat16 [1024], replicated, may hold values from -1.25 to 1.25
- ln2_gain: bfloat16 [1024], replicated, may hold values from 0.5 to 1.5
- ln2_bias: bfloat16 [1024], replicated, may hold values from -1.25 to 1.25
- w_up: bfloat16 [8, 1024, 4096], P('exp', None, 'seq'), may hold values from -0.1875 to 0.1875
- b_up: bfloat16 [8, 4096], P('exp', 'seq'), may hold values from -1.25 to 1.25
- w_down: bfloat16 [8, 4096, 1024], P('exp', 'seq'), may hold values from -0.09375 to 0.09375
- b_down: bfloat16 [8, 1024], P('exp'), may hold values from -1.25 to 1.25
- cotangent: bfloat16 [8, 1024, 1024], P('exp', 'seq'), may hold values from -6 to 6
Outputs:
- output: bfloat16 [8, 1024, 1024], P('exp', 'seq')
- input_grad: float32 [8, 1024, 1024], P('exp', 'seq')
- grad_ln1_gain: float32 [1024], replicated
- grad_ln1_bias: float32 [1024], replicated
- grad_w_query: float32 [1024, 1024], replicated
- grad_b_query: float32 [1024], replicated
- grad_w_key: float32 [1024, 1024], replicated
- grad_w_value: float32 [1024, 1024], replicated
- grad_b_value: float32 [1024], replicated
- grad_w_out: float32 [1024, 1024], replicated
- grad_b_out: float32 [1024], replicated
- grad_ln2_gain: float32 [1024], replicated
- grad_ln2_bias: float32 [1024], replicated
- grad_w_up: float32 [8, 1024, 4096], P('exp', None, 'seq')
- grad_b_up: float32 [8, 4096], P('exp', 'seq')
- grad_w_down: float32 [8, 4096, 1024], P('exp', 'seq')
- grad_b_down: float32 [8, 1024], P('exp', 'seq')
Inputs may be any that keep to these rules, and one draw needn't show every extreme that they name: Each group's 3 lengths sum to 1024. `expert_ids`: among the 256 tokens of one device (aligned blocks along the token dimensions), no expert is named more than 64 times; in some blocks an expert is named exactly 64 times.
All inputs are finite; a program needn't handle non-finite values.
Results may differ from a plain program's by a relative error of at most 0.017.
Values may be sent and summed in bfloat16 or wider, within the bound.
A program may use at most 192 MiB of HBM per device.

v0:
```python
import math

import jax
import jax.numpy as jnp
from jax import lax
from jax.sharding import PartitionSpec as P

HEADS = 16
HEAD_DIM = 64


EPSILON = 1e-05
SCORE_SCALE = 0.125
MASKED_SCORE = -1e30


def norm_layer(values_in, gain_vec, shift_vec):
    center = values_in - jnp.mean(values_in, axis=-1, keepdims=True)
    inv_std = lax.rsqrt(jnp.mean(center * center, axis=-1, keepdims=True) + EPSILON)
    return center * inv_std * gain_vec + shift_vec


def segment_ids(positions, seq_ends):
    return jnp.sum((positions[:, None] >= seq_ends[None, :]).astype(jnp.int32), axis=1)


def visible_pairs(query_pos, query_seg, key_pos, key_seg):
    return ((query_seg[:, None] == key_seg[None, :]) & (key_pos[None, :] <= query_pos[:, None]))[
        None
    ]


def project(left_op, right_op):
    return jnp.dot(left_op, right_op, preferred_element_type=jnp.float32)


def shards(
    tokens,
    lengths,
    expert_ids,
    ln1_gain,
    ln1_bias,
    w_query,
    b_query,
    w_key,
    w_value,
    b_value,
    w_out,
    b_out,
    ln2_gain,
    ln2_bias,
    w_up,
    b_up,
    w_down,
    b_down,
    cotangent,
):
    tok_rows = tokens.shape[1]
    width = tokens.shape[2]
    seq_size = lax.axis_size("seq")
    exp_size = lax.axis_size("exp")
    seq_rank = lax.axis_index("seq")
    seq_ends = jnp.cumsum(lengths[0])
    own_pos = seq_rank * tok_rows + jnp.arange(tok_rows, dtype=jnp.int32)
    own_seg = segment_ids(own_pos, seq_ends)
    inputs = tokens[0].astype(jnp.float32)
    gain_one = ln1_gain.astype(jnp.float32)
    bias_one = ln1_bias.astype(jnp.float32)
    gain_two = ln2_gain.astype(jnp.float32)
    bias_two = ln2_bias.astype(jnp.float32)
    normed_one_low = norm_layer(inputs, gain_one, bias_one).astype(jnp.bfloat16)
    query_low = (project(normed_one_low, w_query) + b_query.astype(jnp.float32)).astype(
        jnp.bfloat16
    )
    keys_low = project(normed_one_low, w_key).astype(jnp.bfloat16)
    values_low = (project(normed_one_low, w_value) + b_value.astype(jnp.float32)).astype(
        jnp.bfloat16
    )
    query_heads = query_low.reshape(tok_rows, HEADS, HEAD_DIM)
    initial = (
        jnp.full((HEADS, tok_rows), MASKED_SCORE, jnp.float32),
        jnp.zeros((HEADS, tok_rows), jnp.float32),
        jnp.zeros((HEADS, tok_rows, HEAD_DIM), jnp.float32),
    )
    key_piece = lax.all_gather(keys_low, "seq", axis=0, tiled=True)
    value_piece = lax.all_gather(values_low, "seq", axis=0, tiled=True)
    piece_len = key_piece.shape[0]
    fold_block_len = math.gcd(piece_len, 512)
    block_count = piece_len // fold_block_len
    key_blocks = key_piece.reshape(block_count, fold_block_len, HEADS, HEAD_DIM)
    value_blocks = value_piece.reshape(block_count, fold_block_len, HEADS, HEAD_DIM)
    offsets = jnp.arange(block_count, dtype=jnp.int32) * fold_block_len

    def block_step(state_now, packed):
        row_max, row_total, accumulated = state_now
        key_blk, value_blk, offset = packed
        key_pos = offset + jnp.arange(fold_block_len, dtype=jnp.int32)
        allowed = visible_pairs(own_pos, own_seg, key_pos, segment_ids(key_pos, seq_ends))
        scores = (
            jnp.einsum("qhd,khd->hqk", query_heads, key_blk, preferred_element_type=jnp.float32)
            * SCORE_SCALE
        )
        masked = jnp.where(allowed, scores, MASKED_SCORE)
        new_max = jnp.maximum(row_max, jnp.max(masked, axis=-1))
        weights = jnp.where(allowed, jnp.exp(masked - new_max[..., None]), 0.0)
        factor = jnp.exp(row_max - new_max)
        row_total = row_total * factor + jnp.sum(weights, axis=-1)
        accumulated = accumulated * factor[..., None] + jnp.einsum(
            "hqk,khd->hqd",
            weights.astype(jnp.bfloat16),
            value_blk,
            preferred_element_type=jnp.float32,
        )
        return ((new_max, row_total, accumulated), None)

    result, _ = lax.scan(block_step, initial, (key_blocks, value_blocks, offsets))
    row_max, row_total, accumulated = result
    attn_heads = accumulated / row_total[..., None]
    attn_low = jnp.transpose(attn_heads, (1, 0, 2)).reshape(tok_rows, width).astype(jnp.bfloat16)
    resid = inputs + project(attn_low, w_out) + b_out.astype(jnp.float32)
    normed_two_low = norm_layer(resid, gain_two, bias_two).astype(jnp.bfloat16)
    experts = exp_size * w_up.shape[0]
    capacity = 2 * tok_rows // experts
    expert_of = expert_ids[0, :, 0]
    onehot = (expert_of[:, None] == jnp.arange(experts, dtype=jnp.int32)[None, :]).astype(jnp.int32)
    slot_of = jnp.sum(onehot * (jnp.cumsum(onehot, axis=0) - onehot), axis=1)
    send_rows = (
        jnp.zeros((experts, capacity, width), jnp.bfloat16)
        .at[expert_of, slot_of]
        .set(normed_two_low)
    )
    received = lax.all_to_all(send_rows, "exp", split_axis=0, concat_axis=0, tiled=True)
    recv_count = experts * capacity
    recv_rows = received.reshape(recv_count, width)
    up_weight = w_up[0]
    up_bias = b_up[0]
    down_weight = w_down[0]
    down_bias = b_down[0].astype(jnp.float32)
    piece_width = width // seq_size
    grad_send = (
        jnp.zeros((experts, capacity, width), jnp.bfloat16).at[expert_of, slot_of].set(cotangent[0])
    )
    gathered = lax.all_gather(recv_rows, "seq", axis=0, tiled=True)
    preact = project(gathered, up_weight) + up_bias.astype(jnp.float32)
    act_low = jax.nn.gelu(preact).astype(jnp.bfloat16)
    part = act_low
    expert_out = (
        lax.psum_scatter(
            project(part, down_weight).astype(jnp.bfloat16), "seq", scatter_dimension=0, tiled=True
        ).astype(jnp.float32)
        + down_bias
    )
    returned = lax.all_to_all(
        expert_out.astype(jnp.bfloat16).reshape(experts, capacity, width),
        "exp",
        split_axis=0,
        concat_axis=0,
        tiled=True,
    )
    grad_recv = lax.all_to_all(grad_send, "exp", split_axis=0, concat_axis=0, tiled=True).reshape(
        recv_count, width
    )
    grad_all = lax.all_gather(grad_recv, "seq", axis=0, tiled=True)
    bias_full = jnp.sum(grad_all.astype(jnp.float32), axis=0)
    grad_b_down = lax.dynamic_slice_in_dim(bias_full, seq_rank * piece_width, piece_width, 0)
    grad_act = jnp.einsum("rd,fd->rf", grad_all, down_weight, preferred_element_type=jnp.float32)
    grad_pre = jax.vjp(jax.nn.gelu, preact)[1](grad_act)[0].astype(jnp.bfloat16)
    grad_w_down = jnp.einsum("rf,rd->fd", act_low, grad_all, preferred_element_type=jnp.float32)
    grad_w_up = jnp.einsum("rd,rf->df", gathered, grad_pre, preferred_element_type=jnp.float32)
    grad_b_up = jnp.sum(grad_pre.astype(jnp.float32), axis=0)
    part = grad_pre
    grad_home = lax.psum_scatter(
        jnp.einsum("rf,df->rd", part, up_weight, preferred_element_type=jnp.float32).astype(
            jnp.bfloat16
        ),
        "seq",
        scatter_dimension=0,
        tiled=True,
    )
    ffn_rows = returned[expert_of, slot_of].astype(jnp.float32)
    output = (resid + ffn_rows).astype(jnp.bfloat16)
    grad_back = lax.all_to_all(
        grad_home.reshape(experts, capacity, width), "exp", split_axis=0, concat_axis=0, tiled=True
    )
    grad_normed_two = grad_back[expert_of, slot_of].astype(jnp.float32)
    _, norm_two_back = jax.vjp(norm_layer, resid, gain_two, bias_two)
    grad_resid_norm, grad_gain_two, grad_bias_two = norm_two_back(grad_normed_two)
    grad_resid = cotangent[0].astype(jnp.float32) + grad_resid_norm
    grad_out_low = grad_resid.astype(jnp.bfloat16)
    grad_w_out = jnp.einsum("qa,qd->ad", attn_low, grad_out_low, preferred_element_type=jnp.float32)
    grad_b_out = jnp.sum(grad_out_low.astype(jnp.float32), axis=0)
    grad_attn_low = jnp.einsum(
        "qd,ad->qa", grad_out_low, w_out, preferred_element_type=jnp.float32
    ).astype(jnp.bfloat16)
    grad_attn_heads = grad_attn_low.reshape(tok_rows, HEADS, HEAD_DIM)
    delta = jnp.sum(
        jnp.transpose(grad_attn_heads.astype(jnp.float32), (1, 0, 2)) * attn_heads, axis=-1
    )
    whole_keys, whole_values = (
        lax.all_gather(keys_low, "seq", axis=0, tiled=True),
        lax.all_gather(values_low, "seq", axis=0, tiled=True),
    )
    group_len = whole_keys.shape[0]
    block_len = math.gcd(group_len, 512)
    block_count = group_len // block_len

    def back_step(grad_query, packed):
        key_blk, value_blk, offset = packed
        key_pos = offset + jnp.arange(block_len, dtype=jnp.int32)
        allowed = visible_pairs(own_pos, own_seg, key_pos, segment_ids(key_pos, seq_ends))
        scores = (
            jnp.einsum("qhd,khd->hqk", query_heads, key_blk, preferred_element_type=jnp.float32)
            * SCORE_SCALE
        )
        masked = jnp.where(allowed, scores, MASKED_SCORE)
        probabilities = (
            jnp.where(allowed, jnp.exp(masked - row_max[..., None]), 0.0) / row_total[..., None]
        )
        probs_low = probabilities.astype(jnp.bfloat16)
        grad_probs = jnp.einsum(
            "qhd,khd->hqk", grad_attn_heads, value_blk, preferred_element_type=jnp.float32
        )
        grad_scores = (probabilities * (grad_probs - delta[..., None])).astype(jnp.bfloat16)
        grad_query = (
            grad_query
            + jnp.einsum("hqk,khd->qhd", grad_scores, key_blk, preferred_element_type=jnp.float32)
            * SCORE_SCALE
        )
        grad_key_blk = (
            jnp.einsum("hqk,qhd->khd", grad_scores, query_heads, preferred_element_type=jnp.float32)
            * SCORE_SCALE
        )
        grad_value_blk = jnp.einsum(
            "hqk,qhd->khd", probs_low, grad_attn_heads, preferred_element_type=jnp.float32
        )
        return (grad_query, (grad_key_blk, grad_value_blk))

    block_offsets = jnp.arange(block_count, dtype=jnp.int32) * block_len
    grad_query, key_value_parts = lax.scan(
        back_step,
        jnp.zeros((tok_rows, HEADS, HEAD_DIM), jnp.float32),
        (
            whole_keys.reshape(block_count, block_len, HEADS, HEAD_DIM),
            whole_values.reshape(block_count, block_len, HEADS, HEAD_DIM),
            block_offsets,
        ),
    )
    grad_keys, grad_values = (
        lax.psum_scatter(
            key_value_parts[0].reshape(group_len, width).astype(jnp.bfloat16),
            "seq",
            scatter_dimension=0,
            tiled=True,
        ).astype(jnp.float32),
        lax.psum_scatter(
            key_value_parts[1].reshape(group_len, width).astype(jnp.bfloat16),
            "seq",
            scatter_dimension=0,
            tiled=True,
        ).astype(jnp.float32),
    )
    grad_query_low = grad_query.reshape(tok_rows, width).astype(jnp.bfloat16)
    grad_keys_low = grad_keys.astype(jnp.bfloat16)
    grad_values_low = grad_values.astype(jnp.bfloat16)
    grad_w_query = jnp.einsum(
        "qa,qd->ad", normed_one_low, grad_query_low, preferred_element_type=jnp.float32
    )
    grad_b_query = jnp.sum(grad_query_low.astype(jnp.float32), axis=0)
    grad_w_key = jnp.einsum(
        "qa,qd->ad", normed_one_low, grad_keys_low, preferred_element_type=jnp.float32
    )
    grad_w_value = jnp.einsum(
        "qa,qd->ad", normed_one_low, grad_values_low, preferred_element_type=jnp.float32
    )
    grad_b_value = jnp.sum(grad_values_low.astype(jnp.float32), axis=0)
    grad_normed_one = (
        (
            jnp.einsum("qd,ad->qa", grad_query_low, w_query, preferred_element_type=jnp.float32)
            + jnp.einsum("qd,ad->qa", grad_keys_low, w_key, preferred_element_type=jnp.float32)
            + jnp.einsum("qd,ad->qa", grad_values_low, w_value, preferred_element_type=jnp.float32)
        )
        .astype(jnp.bfloat16)
        .astype(jnp.float32)
    )
    _, norm_one_back = jax.vjp(norm_layer, inputs, gain_one, bias_one)
    grad_in_norm, grad_gain_one, grad_bias_one = norm_one_back(grad_normed_one)
    input_grad = grad_resid + grad_in_norm
    summed = lax.psum(
        (
            grad_gain_one,
            grad_bias_one,
            grad_w_query,
            grad_b_query,
            grad_w_key,
            grad_w_value,
            grad_b_value,
            grad_w_out,
            grad_b_out,
            grad_gain_two,
            grad_bias_two,
        ),
        ("seq", "exp"),
    )
    return (
        output[None],
        input_grad[None],
        summed[0],
        summed[1],
        summed[2],
        summed[3],
        summed[4],
        summed[5],
        summed[6],
        summed[7],
        summed[8],
        summed[9],
        summed[10],
        grad_w_up[None],
        grad_b_up[None],
        grad_w_down[None],
        grad_b_down[None],
    )


def solution(mesh):
    placed = (
        P("exp", "seq", None),
        P("exp", None),
        P("exp", "seq", None),
        P(),
        P(),
        P(),
        P(),
        P(),
        P(),
        P(),
        P(),
        P(),
        P(),
        P(),
        P("exp", None, "seq"),
        P("exp", "seq"),
        P("exp", "seq", None),
        P("exp", None),
        P("exp", "seq", None),
    )
    return jax.shard_map(
        shards,
        mesh=mesh,
        in_specs=placed,
        out_specs=(
            P("exp", "seq", None),
            P("exp", "seq", None),
            P(),
            P(),
            P(),
            P(),
            P(),
            P(),
            P(),
            P(),
            P(),
            P(),
            P(),
            P("exp", None, "seq"),
            P("exp", "seq"),
            P("exp", "seq", None),
            P("exp", "seq"),
        ),
        check_vma=False,
    )
```

profile of v0, /device:TPU:25, one launch (start us, length us, event | category | flops | bytes accessed | tf_op | source)
XLA Modules:
  0.0 907.8 jit_solution(5939437711801386965)
XLA Ops:
  24.5 27.3 %all-gather.5.cloned.1.call-done = bf16[1024,1024]{1,0:T(8,128)(2,1)} async-done(((bf16[256,1024]{1,0:T(8,128)(2,1)}), bf16[1024,1024]{1,0:T(8,128)(2,1)}) %all-gather.5.cloned.1.call-update) | async-done | bytes 2097168 | tf_op jit(solution)/shard_map/all_gather | solution.py:85
  51.8 6.3 reshape.418
  63.7 25.9 %all-gather.7.cloned.1.call-done = bf16[1024,1024]{1,0:T(8,128)(2,1)} async-done(((bf16[256,1024]{1,0:T(8,128)(2,1)}), bf16[1024,1024]{1,0:T(8,128)(2,1)}) %all-gather.7.cloned.1.call-update) | async-done | bytes 2097168 | tf_op jit(solution)/shard_map/all_gather | solution.py:86
  89.6 6.3 reshape.419
  101.4 19.1 %while.30 = (s32[]{:T(128)}, f32[16,256]{1,0:T(8,128)S(1)}, f32[16,256]{1,0:T(8,128)S(1)}, f32[16,256,64]{1,2,0:T(8,128)}, s32[256]{0:T(256)S(1)}, /*index=5*/s3...) while((s32[]{:T(128)}, f32[16,256]{1,0:T(8,128)S(1)}, ...), condition=%wide.region_8.9_spmd.clone, body=%wide.region_4.8_spmd.clone.sunk | while | flops 565338880 | bytes 47461644 | solution.py:116
  126.8 37.0 %scatter_fusion = bf16[8,64,1024]{2,1,0:T(8,128)(2,1)} fusion(bf16[8,64,1024]{2,1,0:T(8,128)(2,1)} %broadcast.295.clone, s32[256]{0:T(256)S(1)} %bitcast.254, bf16[256,1024]{1,0:T(8,128)(2,1)S(1)} %add_convert_fusion.2), kind=kCustom, calls=%fused_computation.2 | custom fusion | bytes 1574912 | tf_op jit(solution)/shard_map/scatter | solution.py:130
  163.8 29.9 %all_to_all.20 = bf16[8,64,1024]{2,1,0:T(8,128)(2,1)} all-to-all(bf16[8,64,1024]{2,1,0:T(8,128)(2,1)} %scatter_fusion), channel_id=1, replica_groups=mesh['seq'=4,'exp'=8] {'exp'}, dimensions={0} | all-to-all | bytes 2097152 | tf_op jit(solution)/shard_map/all_to_all | solution.py:132
  195.3 37.0 %scatter_fusion.1 = bf16[8,64,1024]{2,1,0:T(8,128)(2,1)} fusion(bf16[8,64,1024]{2,1,0:T(8,128)(2,1)} %broadcast.295.clone.1, s32[256]{0:T(256)S(1)} %bitcast.255, bf16[256,1024]{1,0:T(8,128)(2,1)S(1)} %bitcast.267), kind=kCustom, calls=%fused_computation.3 | custom fusion | bytes 1574912 | tf_op jit(solution)/shard_map/scatter | solution.py:141
  232.3 31.1 %all_to_all.21 = bf16[8,64,1024]{2,1,0:T(8,128)(2,1)} all-to-all(bf16[8,64,1024]{2,1,0:T(8,128)(2,1)} %scatter_fusion.1), channel_id=1, replica_groups=mesh['seq'=4,'exp'=8] {'exp'}, dimensions={0} | all-to-all | bytes 2097152 | tf_op jit(solution)/shard_map/all_to_all | solution.py:160
  263.5 11.1 %fusion.57 = f32[2048,1024]{1,0:T(8,128)} fusion(bf16[2048,1024]{1,0:T(8,128)(2,1)} %all-gather.9.cloned.1.call-done, bf16[1,1024,1024]{2,1,0:T(8,128)(2,1)} %param.37), kind=kOutput, calls=%fused_computation.80 | convolution fusion | flops 4294967296 | bytes 14680064 | tf_op jit(solution)/shard_map/dot_general | solution.py:34
  274.6 42.2 %all-gather.11.cloned.1.call-done = bf16[2048,1024]{1,0:T(8,128)(2,1)} async-done(((bf16[512,1024]{1,0:T(8,128)(2,1)}), bf16[2048,1024]{1,0:T(8,128)(2,1)}) %all-gather.11.cloned.1.call-update) | async-done | bytes 4194320 | tf_op jit(solution)/shard_map/all_gather | solution.py:163
  316.8 13.4 %convert_reduce_fusion.3 = (f32[1024]{0:T(1024)}, bf16[2048,1024]{1,0:T(8,128)(2,1)S(1)}) fusion(f32[2048,1024]{1,0:T(8,128)} %fusion.57, f32[1024]{0:T(1024)S(1)} %bitcast.277, bf16[2048,1024]{1,0:T(8,128)(2,1)} %all-gather.11.cloned.1.call-done, bf16[1,1024,1024]{2,1,0:T(8,128)(2,1)S(1)} %copy-done), kind=kOutput, calls=%fused_computation.70 | convolution fusion | flops 4343200768 | bytes 18882560 | tf_op jit(solution)/shard_map/rd,fd->rf/dot_general | solution.py:166
  332.1 6.2 convolution_convert_fusion
  338.6 11.2 %convolution_convert_fusion.1 = bf16[2048,1024]{1,0:T(8,128)(2,1)} fusion(bf16[1,1024,1024]{2,1,0:T(8,128)(2,1)S(1)} %copy-done, f32[2048,1024]{1,0:T(8,128)} %fusion.57, f32[1024]{0:T(1024)S(1)} %bitcast.278), kind=kOutput, calls=%fused_computation.73 | convolution fusion | flops 4318035968 | bytes 14684160 | tf_op jit(solution)/shard_map/dot_general | solution.py:34
  349.8 41.4 %reduce-scatter.7.cloned.1.call-done = bf16[512,1024]{1,0:T(8,128)(2,1)} async-done(((bf16[2048,1024]{1,0:T(8,128)(2,1)}), bf16[512,1024]{1,0:T(8,128)(2,1)}) %reduce-scatter.7.cloned.1.call-update) | async-done | bytes 1048592 | tf_op jit(solution)/shard_map/reduce_scatter | solution.py:172
  396.6 51.0 %reduce-scatter.5.cloned.1.call-done = bf16[512,1024]{1,0:T(8,128)(2,1)} async-done(((bf16[2048,1024]{1,0:T(8,128)(2,1)}), bf16[512,1024]{1,0:T(8,128)(2,1)}) %reduce-scatter.5.cloned.1.call-update) | async-done | bytes 1048592 | tf_op jit(solution)/shard_map/reduce_scatter | solution.py:148
  460.0 19.7 %all-to-all-done.1 = bf16[8,64,1024]{2,1,0:T(8,128)(2,1)} async-done(((bf16[8,64,1024]{2,1,0:T(8,128)(2,1)}), bf16[8,64,1024]{2,1,0:T(8,128)(2,1)}, u32[]{:S(2)}, u32[]{:S(2)}) %all-to-all-start.1) | async-done | bytes 1048608 | tf_op jit(solution)/shard_map/all_to_all | solution.py:153
  491.4 28.0 %while.31 = (s32[]{:T(128)}, f32[256,16,64]{0,2,1:T(8,128)S(1)}, bf16[2,512,16,64]{1,3,2,0:T(8,128)(2,1)}, bf16[2,512,16,64]{1,3,2,0:T(8,128)(2,1)}, bf16[2,512,...) while((s32[]{:T(128)}, f32[256,16,64]{0,2,1:T(8,128)S(1)}, ...), condition=%wide.region_23.24_spmd.clone, body=%wide.region_21.23_spmd.clone.sunk | while | flops 1362760448 | bytes 99939720 | solution.py:239
  536.8 23.4 %reduce-scatter.11.cloned.1.call-done = bf16[256,1024]{0,1:T(8,128)(2,1)} async-done(((bf16[1024,1024]{0,1:T(8,128)(2,1)}), bf16[256,1024]{0,1:T(8,128)(2,1)}) %reduce-scatter.11.cloned.1.call-update) | async-done | bytes 524304 | tf_op jit(solution)/shard_map/reduce_scatter | solution.py:255
  564.1 35.1 %reduce-scatter.9.cloned.1.call-done = bf16[256,1024]{0,1:T(8,128)(2,1)} async-done(((bf16[1024,1024]{0,1:T(8,128)(2,1)}), bf16[256,1024]{0,1:T(8,128)(2,1)}) %reduce-scatter.9.cloned.1.call-update) | async-done | bytes 524304 | tf_op jit(solution)/shard_map/reduce_scatter | solution.py:249
  606.9 8.6 convolution_bitcast_fusion.1
  615.5 11.7 %convolution_bitcast_fusion = f32[1,1024,1024]{2,1,0:T(8,128)} fusion(bf16[2048,1024]{1,0:T(8,128)(2,1)S(1)} %copy-done.16, f32[2048,1024]{1,0:T(8,128)} %fusion.57, f32[1024]{0:T(1024)S(1)} %bitcast.279), kind=kOutput, calls=%fused_computation.74 | convolution fusion | flops 4315938816 | bytes 16781312 | tf_op jit(solution)/shard_map/rf,rd->fd/dot_general | solution.py:168
  632.6 40.6 %all-reduce = (f32[1024]{0:T(1024)}, f32[1024]{0:T(1024)}, f32[1024]{0:T(1024)}, f32[1024]{0:T(1024)}, f32[1024]{0:T(1024)}, /*index=5*/f32[1024]{0:T(1024)}, f32[1024]{0:T(1024)}) all-reduce(f32[1024]{0:T(1024)S(1)} %get-tuple-element.331, f32[1024]{0:T(1024)S(1)} %get-tuple-element.334, ...), channel_id=1, replica_groups=mesh['seq'=4,'exp'=8] {'seq','exp'}, use_global_device_ids=true, to_apply=%region_29.30 | all-reduce | flops 7168 | bytes 57344 | tf_op jit(solution)/shard_map/psum | solution.py:288
  674.7 212.0 %all-reduce.4.cloned.1.call-done = (f32[1024,1024]{1,0:T(8,128)}, f32[1024,1024]{1,0:T(8,128)}, f32[1024,1024]{1,0:T(8,128)}, f32[1024,1024]{1,0:T(8,128)}) async-done(((f32[1024,1024]{1,0:T(8,128)}, f32[1024,1024]{1,0:T(8,128)}, f32[1024,1024]{1,0:T(8,128)}, f32[1024,1024]{1,0:T(8,128)}), (f32[1024,1024]{1,0:T(8,128)}, f32[1024,1024]{1,0:T(8,128)}, f32[1024,1024]{1,0:T(8,128)}, ...) | async-done | bytes 16777232 | tf_op jit(solution)/shard_map/psum | solution.py:288
  (281 shorter events, 163.9 us)
Async XLA Ops:
  7.2 309.6 %copy-start = (bf16[1,1024,1024]{2,1,0:T(8,128)(2,1)S(1)}, bf16[1,1024,1024]{2,1,0:T(8,128)(2,1)}, u32[]{:S(2)}) copy-start(bf16[1,1024,1024]{2,1,0:T(8,128)(2,1)} %param.39) | copy-start | bytes 6291460
  7.2 44.6 %all-gather.5.cloned.1.call-start = ((), (), s32[]{:S(2)}) async-start(), calls=%async_computation.8 | async-start | bytes 2621440 | tf_op jit(solution)/shard_map/all_gather | solution.py:85
  8.6 11.2 %copy-start.34 = (f32[256]{0:T(256)}, f32[256]{0:T(256)S(1)}, u32[]{:S(2)}) copy-start(f32[256]{0:T(256)S(1)} %broadcast_multiply_fusion.1) | copy-start | bytes 3076
  10.6 9.3 %copy-start.36 = (f32[256]{0:T(256)}, f32[256]{0:T(256)S(1)}, u32[]{:S(2)}) copy-start(f32[256]{0:T(256)S(1)} %fusion.99) | copy-start | bytes 3076
  15.4 74.2 %all-gather.7.cloned.1.call-start = ((), (), s32[]{:S(2)}) async-start(), calls=%async_computation.9 | async-start | bytes 2621440 | tf_op jit(solution)/shard_map/all_gather | solution.py:86
  18.6 244.9 %all-gather.9.cloned.1.call-start = ((), (), s32[]{:S(2)}) async-start(), calls=%async_computation.10 | async-start | bytes 5242880 | tf_op jit(solution)/shard_map/all_gather | solution.py:143
  163.8 31.5 %copy-start.14 = (bf16[1,256,1024]{2,1,0:T(8,128)(2,1)S(1)}, bf16[1,256,1024]{2,1,0:T(8,128)(2,1)}, u32[]{:S(2)}) copy-start(bf16[1,256,1024]{2,1,0:T(8,128)(2,1)} %param.41) | copy-start | bytes 1572868
  193.7 123.2 %all-gather.11.cloned.1.call-start = ((), (), s32[]{:S(2)}) async-start(), calls=%async_computation.12 | async-start | bytes 5242880 | tf_op jit(solution)/shard_map/all_gather | solution.py:163
  195.3 68.2 %copy-start.46 = (bf16[1,1024]{1,0:T(2,128)(2,1)S(1)}, bf16[1,1024]{1,0:T(2,128)(2,1)}, u32[]{:S(2)}) copy-start(bf16[1,1024]{1,0:T(2,128)(2,1)} %param.38) | copy-start | bytes 6148
  263.4 127.8 %reduce-scatter.7.cloned.1.call-start = ((), (), s32[]{:S(2)}) async-start(), calls=%async_computation.13 | async-start | bytes 5242880 | tf_op jit(solution)/shard_map/reduce_scatter | solution.py:172
  263.5 75.1 %copy-start.48 = (f32[1,1024]{1,0:T(1,128)}, f32[1,1024]{1,0:T(1,128)S(1)}, u32[]{:S(2)}) copy-start(f32[1,1024]{1,0:T(1,128)S(1)} %add.267) | copy-start | bytes 12292
  316.8 15.3 %copy-start.56 = (bf16[1,1024,1024]{2,1,0:T(8,128)(2,1)S(1)}, bf16[1,1024,1024]{2,1,0:T(8,128)(2,1)}, u32[]{:S(2)}) copy-start(bf16[1,1024,1024]{2,1,0:T(8,128)(2,1)} %param.37) | copy-start | bytes 6291460
  338.4 109.2 %reduce-scatter.5.cloned.1.call-start = ((), (), s32[]{:S(2)}) async-start(), calls=%async_computation.11 | async-start | bytes 5242880 | tf_op jit(solution)/shard_map/reduce_scatter | solution.py:148
  349.8 46.9 %copy-start.47 = (bf16[1,1024]{1,0:T(2,128)(2,1)S(1)}, bf16[1,1024]{1,0:T(2,128)(2,1)}, u32[]{:S(2)}) copy-start(bf16[1,1024]{1,0:T(2,128)(2,1)} %param.40) | copy-start | bytes 6148
  391.2 58.9 %all-to-all-start.3 = ((bf16[8,64,1024]{2,1,0:T(8,128)(2,1)}), bf16[8,64,1024]{2,1,0:T(8,128)(2,1)S(1)}, u32[]{:S(2)}, u32[]{:S(2)}) async-start(bf16[8,64,1024]{2,1,0:T(8,128)(2,1)} %bitcast.271), calls=%async_computation.5 | async-start | bytes 2097152 | tf_op jit(solution)/shard_map/all_to_all | solution.py:182
  447.6 11.4 %copy-start.6 = (f32[256,1024]{1,0:T(8,128)S(1)}, f32[256,1024]{1,0:T(8,128)}, u32[]{:S(2)}) copy-start(f32[256,1024]{1,0:T(8,128)} %copy-done.5) | copy-start | bytes 3145732
  450.2 29.5 %all-to-all-start.1 = ((bf16[8,64,1024]{2,1,0:T(8,128)(2,1)}), bf16[8,64,1024]{2,1,0:T(8,128)(2,1)}, u32[]{:S(2)}, u32[]{:S(2)}) async-start(bf16[8,64,1024]{2,1,0:T(8,128)(2,1)} %bitcast.269), calls=%async_computation.2 | async-start | bytes 2097152 | tf_op jit(solution)/shard_map/all_to_all | solution.py:153
  455.6 104.6 %reduce-scatter.11.cloned.1.call-start = ((), (), s32[]{:S(2)}) async-start(), calls=%async_computation.15 | async-start | bytes 2621440 | tf_op jit(solution)/shard_map/reduce_scatter | solution.py:255
  525.1 74.1 %reduce-scatter.9.cloned.1.call-start = ((), (), s32[]{:S(2)}) async-start(), calls=%async_computation.14 | async-start | bytes 2621440 | tf_op jit(solution)/shard_map/reduce_scatter | solution.py:249
  530.8 355.9 %all-reduce.4.cloned.1.call-start = ((), (), s32[]{:S(2)}) async-start(), calls=%async_computation.16 | async-start | bytes 33554432 | tf_op jit(solution)/shard_map/psum | solution.py:288
  615.5 14.4 %copy-start.24 = (bf16[256,1024]{0,1:T(8,128)(2,1)S(1)}, bf16[256,1024]{0,1:T(8,128)(2,1)}, u32[]{:S(2)}) copy-start(bf16[256,1024]{0,1:T(8,128)(2,1)} %reduce-scatter.11.cloned.1.call-done) | copy-start | bytes 1572868
  631.0 42.3 %copy-start.11 = (f32[256,1024]{1,0:T(8,128)S(1)}, f32[256,1024]{1,0:T(8,128)}, u32[]{:S(2)}) copy-start(f32[256,1024]{1,0:T(8,128)} %copy-done.10) | copy-start | bytes 3145732
  631.0 42.3 %copy-start.15 = (bf16[1,256,1024]{2,1,0:T(8,128)(2,1)S(1)}, bf16[1,256,1024]{2,1,0:T(8,128)(2,1)}, u32[]{:S(2)}) copy-start(bf16[1,256,1024]{2,1,0:T(8,128)(2,1)} %param.41) | copy-start | bytes 1572868
  631.0 42.3 %copy-start.45 = (f32[256]{0:T(256)S(1)}, f32[256]{0:T(256)}, u32[]{:S(2)}) copy-start(f32[256]{0:T(256)} %copy-done.44) | copy-start | bytes 3076
  (56 other events, 204.5 us)
Sparse Core Ops, SparseCore 0:
  15.5 36.2 all-gather.4
  54.2 35.2 all-gather.6
  193.8 52.6 all-gather.8
  263.6 53.2 all-gather.10
  338.5 52.6 reduce-scatter.6
  394.9 52.6 reduce-scatter.4
  525.2 34.9 reduce-scatter.10
  564.0 35.1 reduce-scatter.8
  606.8 279.8 all-reduce.3
where the time goes:
time: 925 us; the launch traced here: 908 us
  waiting for transfers between devices  478 us (52%)
  local copies, waits for them, and re-layouts  151 us (16%)
  matrix products  121 us (13%)
  blocking collectives  102 us (11%)
  other arithmetic  29.5 us (3%)
  between operations  14.7 us (2%)
  starting transfers between devices  11.8 us (1%)
    psum x1, waiting for transfers between devices, shards(): lax.psum((grad_gain_one, grad_bias_one, grad_w_query, grad_b_query, grad_...  212 us
    reduce_scatter x1, waiting for transfers between devices, shards(): lax.psum_scatter(project(part, down_weight).astype(jnp.bfloat16), 'seq',...  51 us
    all_gather x1, waiting for transfers between devices, shards(): grad_all = lax.all_gather(grad_recv, 'seq', axis=0, tiled=True)  42.2 us
    reduce_scatter x1, waiting for transfers between devices, shards(): lax.psum_scatter(jnp.einsum('rf,df->rd', part, up_weight, preferred_eleme...  41.4 us
    psum x1, blocking collectives, shards(): lax.psum((grad_gain_one, grad_bias_one, grad_w_query, grad_b_query, grad_...  40.6 us
    scatter x1, local copies, waits for them, and re-layouts, shards(): jnp.zeros((experts, capacity, width), jnp.bfloat16).at[expert_of, slot_of]  37 us
    scatter x1, local copies, waits for them, and re-layouts, shards(): send_rows = jnp.zeros((experts, capacity, width), jnp.bfloat16).at[expert...  37 us
    reduce_scatter x1, waiting for transfers between devices, shards(): lax.psum_scatter(key_value_parts[0].reshape(group_len, width).astype(jnp....  35.1 us
  transfers between devices with their start and end apart: 11, of which 9 were waited for; matrix products, arithmetic and copies ran while one was open for 15% of the time, Pallas kernels for 0%

commit v1 on v0

--- a/solution.py
+++ b/solution.py
@@ -1,9 +1,13 @@
+import functools
 import math
 
 import jax
 import jax.numpy as jnp
 from jax import lax
+from jax.experimental import pallas as pl
+from jax.experimental.pallas import tpu as pltpu
 from jax.sharding import PartitionSpec as P
+
 
 HEADS = 16
 HEAD_DIM = 64
@@ -32,6 +36,501 @@
 
 def project(left_op, right_op):
     return jnp.dot(left_op, right_op, preferred_element_type=jnp.float32)
+
+
+MESH = pl.DeviceIdType.MESH
+F32 = jnp.float32
+BF16 = jnp.bfloat16
+VMEM_LIMIT = 60 * 2**20
+
+
+def dot(a, b, dims=((1,), (0,))):
+    return lax.dot_general(a, b, (dims, ((), ())), preferred_element_type=F32)
+
+
+class Place:
+    def __init__(self, n_exp):
+        self.n_exp = n_exp
+        self.s = lax.axis_index("seq")
+        self.e = lax.axis_index("exp")
+        low = lax.rem(self.s, 2)
+        high = lax.div(self.s, 2)
+        self.near = high * 2 + (1 - low)
+        self.far = (1 - high) * 2 + low
+        self.diag = (1 - high) * 2 + (1 - low)
+        self.core = lax.rem(self.e, 2)
+        self.chip = lax.div(self.e, 2)
+
+    def peer(self, step, way):
+        chips = self.n_exp // 2
+        hop = lax.div(step, 2)
+        if chips == 4:
+            hop = hop + lax.div(hop, 2) * (5 - 2 * hop)
+        chip = lax.rem(self.chip + way * hop + chips, chips)
+        return chip * 2 + lax.rem(self.core + step, 2)
+
+    def greet(self, seq=True, exp=True):
+        barrier = pltpu.get_barrier_semaphore()
+        count = 0
+        if seq:
+            for other in (self.near, self.far):
+                pl.semaphore_signal(barrier, inc=1, device_id=(other, self.e), device_id_type=MESH)
+            count += 2
+        if exp:
+
+            def tell(step, carry):
+                pl.semaphore_signal(
+                    barrier, inc=1, device_id=(self.s, self.peer(step, 1)), device_id_type=MESH
+                )
+                return carry
+
+            lax.fori_loop(1, self.n_exp, tell, 0)
+            count += self.n_exp - 1
+        pl.semaphore_wait(barrier, count)
+
+    def to_seq(self, src, dst, send_sem, recv_sem, other):
+        return pltpu.make_async_remote_copy(
+            src_ref=src, dst_ref=dst, send_sem=send_sem, recv_sem=recv_sem,
+            device_id=(other, self.e), device_id_type=MESH,
+        )
+
+    def to_exp(self, src, dst, send_sem, recv_sem, other):
+        return pltpu.make_async_remote_copy(
+            src_ref=src, dst_ref=dst, send_sem=send_sem, recv_sem=recv_sem,
+            device_id=(self.s, other), device_id_type=MESH,
+        )
+
+
+class Dispatch:
+    def __init__(self, place, send, held, exp_sems, seq_sems):
+        self.place, self.send, self.held = place, send, held
+        self.exp_send, self.exp_recv = exp_sems
+        self.seq_send, self.seq_recv = seq_sems
+        self.cap = send.shape[1]
+
+    @staticmethod
+    def scratch(n_exp):
+        return [
+            pltpu.SemaphoreType.DMA((n_exp,)),
+            pltpu.SemaphoreType.DMA((n_exp,)),
+            pltpu.SemaphoreType.DMA((n_exp, 6)),
+            pltpu.SemaphoreType.DMA((n_exp, 6)),
+        ]
+
+    def _exp(self, step):
+        p = self.place
+        other = p.peer(step, -1)
+        return p.to_exp(
+            self.send.at[other], self.held.at[step, p.s], self.exp_send.at[step], self.exp_recv.at[step], other
+        )
+
+    def _seq(self, step, owner, half, lane, other):
+        p = self.place
+        rows = pl.ds(half * (self.cap // 2), self.cap // 2)
+        part = self.held.at[step, owner, rows]
+        return p.to_seq(part, part, self.seq_send.at[step, lane], self.seq_recv.at[step, lane], other)
+
+    def copies(self, step, lanes=range(6)):
+        p = self.place
+        spec = (
+            (p.s, 0, p.near),
+            (p.s, 1, p.far),
+            (p.s, 1, p.near),
+            (p.s, 0, p.far),
+            (p.near, 0, p.far),
+            (p.far, 1, p.near),
+        )
+        return [self._seq(step, spec[n][0], spec[n][1], n, spec[n][2]) for n in lanes]
+
+    def start_exp(self, step):
+        self._exp(step).start()
+
+    def own(self):
+        p = self.place
+        self.held[0, p.s] = self.send[p.e]
+
+    def start_seq(self, step):
+        @pl.when(step > 0)
+        def _():
+            self._exp(step).wait_recv()
+
+        for c in self.copies(step, range(4)):
+            c.start()
+
+    def relay(self, step):
+        for c, out in zip(self.copies(step, (0, 1)), self.copies(step, (4, 5))):
+            c.wait_recv()
+            out.start()
+
+    def arrived(self, step):
+        for c in self.copies(step, range(2, 6)):
+            c.wait_recv()
+
+    def drain(self):
+        def body(step, carry):
+            for c in self.copies(step):
+                c.wait_send()
+
+            @pl.when(step > 0)
+            def _():
+                self._exp(step).wait_send()
+
+            return carry
+
+        lax.fori_loop(0, self.place.n_exp, body, 0)
+
+
+class Combine:
+    def __init__(self, place, part, passing, landing, total, back, seq_sems, exp_sems, slots):
+        self.place, self.part, self.passing, self.landing = place, part, passing, landing
+        self.total, self.back, self.slots = total, back, slots
+        self.seq_send, self.seq_recv = seq_sems
+        self.exp_send, self.exp_recv = exp_sems
+        self.cap = back.shape[1]
+        self.half = self.cap // 2
+
+    @staticmethod
+    def scratch(n_exp, cap, width):
+        return [
+            pltpu.VMEM((n_exp, 2, cap // 2, width), BF16),
+            pltpu.VMEM((n_exp, 4, cap // 2, width), BF16),
+            pltpu.VMEM((n_exp, cap, width), BF16),
+            pltpu.SemaphoreType.DMA((n_exp, 6)),
+            pltpu.SemaphoreType.DMA((n_exp, 6)),
+            pltpu.SemaphoreType.DMA((n_exp,)),
+            pltpu.SemaphoreType.DMA((n_exp,)),
+        ]
+
+    def _slot(self, step):
+        return lax.rem(step, self.slots)
+
+    def _piece(self, step, owner, half):
+        return self.part.at[self._slot(step), owner, pl.ds(half * self.half, self.half)]
+
+    def _seq(self, src, dst, step, lane, other):
+        return self.place.to_seq(
+            src, dst, self.seq_send.at[step, lane], self.seq_recv.at[step, lane], other
+        )
+
+    def copies(self, step, lanes=range(6)):
+        p = self.place
+        spec = (
+            (p.diag, 0, self.passing, 0, p.near),
+            (p.diag, 1, self.passing, 1, p.far),
+            (p.near, 0, self.landing, 0, p.near),
+            (p.far, 1, self.landing, 3, p.far),
+            (p.far, 0, self.landing, 2, p.far),
+            (p.near, 1, self.landing, 1, p.near),
+        )
+        made = []
+        for n in lanes:
+            owner, half, buffer, at, other = spec[n]
+            made.append(self._seq(self._piece(step, owner, half), buffer.at[step, at], step, n, other))
+        return made
+
+    def start(self, step):
+        for c in self.copies(step, range(4)):
+            c.start()
+
+    def pass_on(self, step):
+        p = self.place
+        slot = self._slot(step)
+        came, out = self.copies(step, (0, 1)), self.copies(step, (4, 5))
+        for n, owner in enumerate((p.far, p.near)):
+            rows = pl.ds(n * self.half, self.half)
+            came[n].wait_recv()
+            self.part[slot, owner, rows] = (
+                self.part[slot, owner, rows].astype(F32) + self.passing[step, n].astype(F32)
+            ).astype(BF16)
+            out[n].start()
+
+    def _exp(self, step):
+        p = self.place
+        other = p.peer(step, 1)
+        return p.to_exp(
+            self.total.at[step], self.back.at[p.e], self.exp_send.at[step], self.exp_recv.at[step], other
+        )
+
+    def finish(self, step, bias=None):
+        p = self.place
+        slot = self._slot(step)
+        copies = self.copies(step)
+        for c in copies[2:]:
+            c.wait_recv()
+        for half in range(2):
+            rows = pl.ds(half * self.half, self.half)
+            value = (
+                self.part[slot, p.s, rows].astype(F32)
+                + self.landing[step, half].astype(F32)
+                + self.landing[step, 2 + half].astype(F32)
+            )
+            if bias is not None:
+                value = value + bias
+            self.total[step, rows] = value.astype(BF16)
+        for c in copies:
+            c.wait_send()
+
+        @pl.when(step > 0)
+        def _():
+            self._exp(step).start()
+
+        @pl.when(step == 0)
+        def _():
+            self.back[p.e] = self.total[0]
+
+    def drain(self):
+        p = self.place
+
+        def body(step, carry):
+            c = self._exp(step)
+            c.wait_send()
+            c.wait_recv()
+            return carry
+
+        lax.fori_loop(1, p.n_exp, body, 0)
+
+
+def dispatch_rows(send, collective_id):
+    n_exp, cap, width = send.shape
+
+    def kernel(send, held, *sems):
+        p = Place(n_exp)
+        p.greet()
+        d = Dispatch(p, send, held, sems[0:2], sems[2:4])
+        d.own()
+
+        d.start_seq(0)
+        for step in range(1, n_exp):
+            d.start_exp(step)
+
+        def loop(t, carry):
+            @pl.when(t < n_exp)
+            def _():
+                d.start_seq(t)
+
+            d.relay(t - 1)
+
+            @pl.when(t >= 2)
+            def _():
+                d.arrived(t - 2)
+
+            return carry
+
+        lax.fori_loop(1, n_exp + 1, loop, 0)
+        d.arrived(n_exp - 1)
+        d.drain()
+
+    return pl.pallas_call(
+        kernel,
+        out_shape=jax.ShapeDtypeStruct((n_exp, 4, cap, width), BF16),
+        in_specs=[pl.BlockSpec(memory_space=pltpu.VMEM)],
+        out_specs=pl.BlockSpec(memory_space=pltpu.VMEM),
+        scratch_shapes=Dispatch.scratch(n_exp),
+        compiler_params=pltpu.CompilerParams(
+            collective_id=collective_id, has_side_effects=True, vmem_limit_bytes=VMEM_LIMIT
+        ),
+        name="dispatch_rows",
+    )(send)
+
+
+def combine_rows(part, bias, collective_id):
+    n_exp, _, cap, width = part.shape
+
+    def kernel(part_in, bias_ref, back, part, load_sem, passing, landing, total, *sems):
+        p = Place(n_exp)
+
+        def load(step):
+            return pltpu.make_async_copy(part_in.at[step], part.at[step], load_sem.at[step])
+
+        for step in range(n_exp):
+            load(step).start()
+        p.greet()
+        c = Combine(p, part, passing, landing, total, back, sems[0:2], sems[2:4], n_exp)
+        bias_row = bias_ref[...].astype(F32)
+
+        def loop(t, carry):
+            @pl.when(t < n_exp)
+            def _():
+                load(t).wait()
+                c.start(t)
+
+            @pl.when((t >= 2) & (t < n_exp + 2))
+            def _():
+                c.pass_on(t - 2)
+
+            @pl.when(t >= 4)
+            def _():
+                c.finish(t - 4, bias_row)
+
+            return carry
+
+        lax.fori_loop(0, n_exp + 4, loop, 0)
+        c.drain()
+
+    return pl.pallas_call(
+        kernel,
+        out_shape=jax.ShapeDtypeStruct((n_exp, cap, width), BF16),
+        in_specs=[pl.BlockSpec(memory_space=pl.ANY), pl.BlockSpec(memory_space=pltpu.VMEM)],
+        out_specs=pl.BlockSpec(memory_space=pltpu.VMEM),
+        scratch_shapes=[
+            pltpu.VMEM((n_exp, 4, cap, width), BF16),
+            pltpu.SemaphoreType.DMA((n_exp,)),
+        ]
+        + Combine.scratch(n_exp, cap, width),
+        compiler_params=pltpu.CompilerParams(
+            collective_id=collective_id, has_side_effects=True, vmem_limit_bytes=VMEM_LIMIT
+        ),
+        name="combine_rows",
+    )(part, bias)
+
+
+GELU_A = math.sqrt(2.0 / math.pi)
+GELU_B = 0.044715
+
+
+def ffn_both(send, cot_rows, w_up, b_up, w_down, collective_id):
+    n_exp, cap, width = send.shape
+    hidden = w_up.shape[1]
+    rows = 4 * cap
+    block = min(512, hidden)
+    slots = 4
+
+    def kernel(send, cot_in, wu_in, bu_ref, wd_in, back, dwu_out, dwd_out, dbu_out, gsum_out, ffn_out,
+               held, cot, wu, wd, part, ffn, dwu, dwd, local_sems, ffn_sems, out_sems, *rest):
+        p = Place(n_exp)
+        loads = [
+            pltpu.make_async_copy(wu_in, wu, local_sems.at[0]),
+            pltpu.make_async_copy(wd_in, wd, local_sems.at[1]),
+            pltpu.make_async_copy(cot_in, cot, local_sems.at[2]),
+        ]
+        for c in loads:
+            c.start()
+        p.greet()
+        d = Dispatch(p, send, held, rest[0:2], rest[2:4])
+        passing, landing, total = rest[4:7]
+        c = Combine(p, part, passing, landing, total, back, rest[7:9], rest[9:11], slots)
+        d.own()
+        d.start_seq(0)
+        for step in range(1, n_exp):
+            d.start_exp(step)
+        dwu[...] = jnp.zeros_like(dwu)
+        dwd[...] = jnp.zeros_like(dwd)
+        dbu_out[...] = jnp.zeros_like(dbu_out)
+        gsum_out[...] = jnp.zeros_like(gsum_out)
+
+        def store(step):
+            slot = lax.rem(step, 2)
+            return pltpu.make_async_copy(ffn.at[slot], ffn_out.at[step], ffn_sems.at[slot])
+
+        def compute(step):
+            x = held[step].reshape(rows, width)
+            g = cot[step].reshape(rows, width)
+            gsum_out[...] += jnp.sum(g.astype(F32), axis=0, keepdims=True)
+            y = jnp.zeros((rows, width), F32)
+            gx = jnp.zeros((rows, width), F32)
+            for k in range(hidden // block):
+                cols = pl.ds(k * block, block)
+                wu_k, wd_k = wu[:, cols], wd[cols, :]
+                pre = dot(x, wu_k) + bu_ref[:, cols].astype(F32)
+                g_act = dot(g, wd_k, ((1,), (1,)))
+                sq = pre * pre
+                th = jnp.tanh(GELU_A * pre * (1.0 + GELU_B * sq))
+                half = 0.5 * (1.0 + th)
+                act = (pre * half).astype(BF16)
+                slope = half + 0.5 * pre * (1.0 - th * th) * (GELU_A * (1.0 + 3.0 * GELU_B * sq))
+                g_pre32 = g_act * slope
+                g_pre = g_pre32.astype(BF16)
+                dbu_out[:, cols] += jnp.sum(g_pre.astype(F32), axis=0, keepdims=True)
+                y = y + dot(act, wd_k)
+                gx = gx + dot(g_pre, wu_k, ((1,), (1,)))
+                dwu[:, cols] += dot(x, g_pre, ((0,), (0,)))
+                dwd[cols, :] += dot(act, g, ((0,), (0,)))
+            part[lax.rem(step, slots)] = gx.astype(BF16).reshape(4, cap, width)
+
+            @pl.when(step >= 2)
+            def _():
+                store(step - 2).wait()
+
+            ffn[lax.rem(step, 2)] = y.astype(BF16).reshape(4, cap, width)
+            store(step).start()
+
+        def loop(t, carry):
+            @pl.when(t < n_exp)
+            def _():
+                d.start_seq(t)
+
+            @pl.when(t <= n_exp)
+            def _():
+                d.relay(t - 1)
+
+            @pl.when((t >= 3) & (t <= n_exp + 2))
+            def _():
+                c.pass_on(t - 3)
+
+            @pl.when(t >= 4)
+            def _():
+                c.finish(t - 4)
+
+            @pl.when(t == 2)
+            def _():
+                for load in loads:
+                    load.wait()
+
+            @pl.when((t >= 2) & (t <= n_exp + 1))
+            def _():
+                d.arrived(t - 2)
+                compute(t - 2)
+                c.start(t - 2)
+
+            @pl.when(t == n_exp + 1)
+            def _():
+                pltpu.make_async_copy(dwu, dwu_out, out_sems.at[0]).start()
+                pltpu.make_async_copy(dwd, dwd_out, out_sems.at[1]).start()
+
+            return carry
+
+        lax.fori_loop(1, n_exp + 4, loop, 0)
+        d.drain()
+        c.drain()
+        store(n_exp - 2).wait()
+        store(n_exp - 1).wait()
+        pltpu.make_async_copy(dwu, dwu_out, out_sems.at[0]).wait()
+        pltpu.make_async_copy(dwd, dwd_out, out_sems.at[1]).wait()
+
+    vmem = pl.BlockSpec(memory_space=pltpu.VMEM)
+    hbm = pl.BlockSpec(memory_space=pl.ANY)
+    return pl.pallas_call(
+        kernel,
+        out_shape=[
+            jax.ShapeDtypeStruct((n_exp, cap, width), BF16),
+            jax.ShapeDtypeStruct((width, hidden), F32),
+            jax.ShapeDtypeStruct((hidden, width), F32),
+            jax.ShapeDtypeStruct((1, hidden), F32),
+            jax.ShapeDtypeStruct((1, width), F32),
+            jax.ShapeDtypeStruct((n_exp, 4, cap, width), BF16),
+        ],
+        in_specs=[vmem, hbm, hbm, vmem, hbm],
+        out_specs=[vmem, hbm, hbm, vmem, vmem, hbm],
+        scratch_shapes=[
+            pltpu.VMEM((n_exp, 4, cap, width), BF16),
+            pltpu.VMEM((n_exp, 4, cap, width), BF16),
+            pltpu.VMEM((width, hidden), BF16),
+            pltpu.VMEM((hidden, width), BF16),
+            pltpu.VMEM((slots, 4, cap, width), BF16),
+            pltpu.VMEM((2, 4, cap, width), BF16),
+            pltpu.VMEM((width, hidden), F32),
+            pltpu.VMEM((hidden, width), F32),
+            pltpu.SemaphoreType.DMA((3,)),
+            pltpu.SemaphoreType.DMA((2,)),
+            pltpu.SemaphoreType.DMA((2,)),
+        ]
+        + Dispatch.scratch(n_exp)
+        + Combine.scratch(n_exp, cap, width),
+        compiler_params=pltpu.CompilerParams(
+            collective_id=collective_id, has_side_effects=True, vmem_limit_bytes=VMEM_LIMIT
+        ),
+        name="ffn_both",
+    )(send, cot_rows, w_up, b_up, w_down)
 
 
 def shards(
@@ -124,65 +623,29 @@
     expert_of = expert_ids[0, :, 0]
     onehot = (expert_of[:, None] == jnp.arange(experts, dtype=jnp.int32)[None, :]).astype(jnp.int32)
     slot_of = jnp.sum(onehot * (jnp.cumsum(onehot, axis=0) - onehot), axis=1)
-    send_rows = (
-        jnp.zeros((experts, capacity, width), jnp.bfloat16)
-        .at[expert_of, slot_of]
-        .set(normed_two_low)
-    )
-    received = lax.all_to_all(send_rows, "exp", split_axis=0, concat_axis=0, tiled=True)
-    recv_count = experts * capacity
-    recv_rows = received.reshape(recv_count, width)
-    up_weight = w_up[0]
-    up_bias = b_up[0]
-    down_weight = w_down[0]
-    down_bias = b_down[0].astype(jnp.float32)
+    place_of = expert_of * capacity + slot_of
+    pick = (
+        place_of[:, None] == jnp.arange(experts * capacity, dtype=jnp.int32)[None, :]
+    ).astype(jnp.bfloat16)
+
+    def scatter_rows(rows):
+        laid = jnp.einsum("ts,td->sd", pick, rows, preferred_element_type=jnp.float32)
+        return laid.astype(jnp.bfloat16).reshape(experts, capacity, width)
+
+    def collect_rows(laid):
+        return project(pick, laid.reshape(experts * capacity, width))
+
+    cot_rows = dispatch_rows(scatter_rows(cotangent[0]), 0)
+    grad_back, grad_w_up, grad_w_down, grad_b_up, bias_full, ffn_part = ffn_both(
+        scatter_rows(normed_two_low), cot_rows, w_up[0], b_up, w_down[0], 1
+    )
+    returned = combine_rows(ffn_part, b_down, 2)
     piece_width = width // seq_size
-    grad_send = (
-        jnp.zeros((experts, capacity, width), jnp.bfloat16).at[expert_of, slot_of].set(cotangent[0])
-    )
-    gathered = lax.all_gather(recv_rows, "seq", axis=0, tiled=True)
-    preact = project(gathered, up_weight) + up_bias.astype(jnp.float32)
-    act_low = jax.nn.gelu(preact).astype(jnp.bfloat16)
-    part = act_low
-    expert_out = (
-        lax.psum_scatter(
-            project(part, down_weight).astype(jnp.bfloat16), "seq", scatter_dimension=0, tiled=True
-        ).astype(jnp.float32)
-        + down_bias
-    )
-    returned = lax.all_to_all(
-        expert_out.astype(jnp.bfloat16).reshape(experts, capacity, width),
-        "exp",
-        split_axis=0,
-        concat_axis=0,
-        tiled=True,
-    )
-    grad_recv = lax.all_to_all(grad_send, "exp", split_axis=0, concat_axis=0, tiled=True).reshape(
-        recv_count, width
-    )
-    grad_all = lax.all_gather(grad_recv, "seq", axis=0, tiled=True)
-    bias_full = jnp.sum(grad_all.astype(jnp.float32), axis=0)
-    grad_b_down = lax.dynamic_slice_in_dim(bias_full, seq_rank * piece_width, piece_width, 0)
-    grad_act = jnp.einsum("rd,fd->rf", grad_all, down_weight, preferred_element_type=jnp.float32)
-    grad_pre = jax.vjp(jax.nn.gelu, preact)[1](grad_act)[0].astype(jnp.bfloat16)
-    grad_w_down = jnp.einsum("rf,rd->fd", act_low, grad_all, preferred_element_type=jnp.float32)
-    grad_w_up = jnp.einsum("rd,rf->df", gathered, grad_pre, preferred_element_type=jnp.float32)
-    grad_b_up = jnp.sum(grad_pre.astype(jnp.float32), axis=0)
-    part = grad_pre
-    grad_home = lax.psum_scatter(
-        jnp.einsum("rf,df->rd", part, up_weight, preferred_element_type=jnp.float32).astype(
-            jnp.bfloat16
-        ),
-        "seq",
-        scatter_dimension=0,
-        tiled=True,
-    )
-    ffn_rows = returned[expert_of, slot_of].astype(jnp.float32)
+    grad_b_up = grad_b_up[0]
+    grad_b_down = lax.dynamic_slice_in_dim(bias_full[0], seq_rank * piece_width, piece_width, 0)
+    ffn_rows = collect_rows(returned)
     output = (resid + ffn_rows).astype(jnp.bfloat16)
-    grad_back = lax.all_to_all(
-        grad_home.reshape(experts, capacity, width), "exp", split_axis=0, concat_axis=0, tiled=True
-    )
-    grad_normed_two = grad_back[expert_of, slot_of].astype(jnp.float32)
+    grad_normed_two = collect_rows(grad_back)
     _, norm_two_back = jax.vjp(norm_layer, resid, gain_two, bias_two)
     grad_resid_norm, grad_gain_two, grad_bias_two = norm_two_back(grad_normed_two)
     grad_resid = cotangent[0].astype(jnp.float32) + grad_resid_norm

time: 925 us -> 706 us (0.76)
  the two profiles are of different devices: /device:TPU:25 before, /device:TPU:0 now
where the time goes in v1:
time: 706 us; the launch traced here: 695 us
  waiting for transfers between devices  247 us (35%)
  Pallas kernels  228 us (32%)
  local copies, waits for them, and re-layouts  75.8 us (11%)
  matrix products  68 us (10%)
  blocking collectives  39.3 us (6%)
  other arithmetic  20.4 us (3%)
  between operations  14.9 us (2%)
    psum x1, waiting for transfers between devices, shards(): lax.psum((grad_gain_one, grad_bias_one, grad_w_query, grad_b_query, grad_...  177 us
    pallas_call x1, Pallas kernels, ffn_both(): pl.pallas_call(kernel, out_shape=[jax.ShapeDtypeStruct((n_exp, cap, width...  89.6 us
    pallas_call x1, Pallas kernels, combine_rows(): pl.pallas_call(kernel, out_shape=jax.ShapeDtypeStruct((n_exp, cap, width)...  81.9 us
    pallas_call x1, Pallas kernels, dispatch_rows(): pl.pallas_call(kernel, out_shape=jax.ShapeDtypeStruct((n_exp, 4, cap, wid...  57 us
    unnamed x93, local copies, waits for them, and re-layouts  40.1 us
    psum x1, blocking collectives, shards(): lax.psum((grad_gain_one, grad_bias_one, grad_w_query, grad_b_query, grad_...  39.3 us
    reduce_scatter x1, waiting for transfers between devices, shards(): lax.psum_scatter(key_value_parts[0].reshape(group_len, width).astype(jnp....  35 us
    reduce_scatter x1, waiting for transfers between devices, shards(): lax.psum_scatter(key_value_parts[1].reshape(group_len, width).astype(jnp....  24 us
  transfers between devices with their start and end apart: 5, of which 4 were waited for; matrix products, arithmetic and copies ran while one was open for 7% of the time, Pallas kernels for 20%

profile of v1, /device:TPU:0, one launch (start us, length us, event | category | flops | bytes accessed | tf_op | source)
XLA Modules:
  0.0 694.8 jit_solution(544207137124172830)
XLA Ops:
  11.4 3.4 convolution_convert_fusion.3
  17.7 3.1 fusion.50
  24.8 57.0 %dispatch_rows.1.cot_in = bf16[8,4,64,1024]{3,2,1,0:T(8,128)(2,1)} custom-call(bf16[8,64,1024]{2,1,0:T(8,128)(2,1)} %bitcast.232), custom_call_target="tpu_custom_call" | custom-call | tf_op jit(solution)/shard_map/dispatch_rows/pallas_call | solution.py:323
  81.9 6.3 reshape.361
  88.2 5.7 copy.69
  93.9 11.2 %all-gather.5.cloned.1.call-done = bf16[1024,1024]{1,0:T(8,128)(2,1)} async-done(((bf16[256,1024]{1,0:T(8,128)(2,1)}), bf16[1024,1024]{1,0:T(8,128)(2,1)}) %all-gather.5.cloned.1.call-update) | async-done | bytes 2097168 | tf_op jit(solution)/shard_map/all_gather | solution.py:585
  105.1 6.3 reshape.362
  111.5 5.4 copy.70
  116.9 19.2 %while.30 = (s32[]{:T(128)}, f32[16,256]{1,0:T(8,128)S(1)}, f32[16,256]{1,0:T(8,128)S(1)}, f32[16,256,64]{1,2,0:T(8,128)}, s32[256]{0:T(256)S(1)}, /*index=5*/s3...) while((s32[]{:T(128)}, f32[16,256]{1,0:T(8,128)S(1)}, ...), condition=%wide.region_8.9_spmd.clone, body=%wide.region_4.8_spmd.clone.sunk | while | flops 565338880 | bytes 47461644 | solution.py:615
  142.6 89.6 %ffn_both.1 = (bf16[8,64,1024]{2,1,0:T(8,128)(2,1)}, f32[1024,1024]{1,0:T(8,128)}, f32[1024,1024]{1,0:T(8,128)}, f32[1,1024]{1,0:T(1,128)}, f32[1,1024]{1,0:T(1,128)}, /*index=5*/bf16[8,4,64,1024]{3,2,1,0:T(8,128)(2,1)}) custom-call(bf16[8,64,1024]{2,1,0:T(8,128)(2,1)} %bitcast.231, bf16[8,4,64,1024]{3,2,1,0:T(8,128)(2,1)} %dispatch_rows.1.cot_in, ...), custom_call_target="tpu_custom_call" | custom-call | tf_op jit(solution)/shard_map/ffn_both/pallas_call | solution.py:502
  241.0 28.3 %while.31 = (s32[]{:T(128)}, f32[256,16,64]{0,2,1:T(8,128)}, bf16[2,512,16,64]{1,3,2,0:T(8,128)(2,1)}, bf16[2,512,16,64]{1,3,2,0:T(8,128)(2,1)}, bf16[2,512,16,6...) while((s32[]{:T(128)}, f32[256,16,64]{0,2,1:T(8,128)}, ...), condition=%wide.region_19.20_spmd.clone, body=%wide.region_17.19_spmd.clone.sunk | while | flops 1362760448 | bytes 108328392 | solution.py:702
  242.8 4.0 fusion.168
  256.9 4.0 fusion.168
  269.4 3.8 copy.75
  275.1 3.8 copy.74
  281.4 4.1 fusion.103
  288.5 24.0 %reduce-scatter.5.cloned.1.call-done = bf16[256,1024]{0,1:T(8,128)(2,1)} async-done(((bf16[1024,1024]{0,1:T(8,128)(2,1)}), bf16[256,1024]{0,1:T(8,128)(2,1)}) %reduce-scatter.5.cloned.1.call-update) | async-done | bytes 524304 | tf_op jit(solution)/shard_map/reduce_scatter | solution.py:718
  312.5 3.9 fusion.92
  316.4 35.0 %reduce-scatter.3.cloned.1.call-done = bf16[256,1024]{0,1:T(8,128)(2,1)} async-done(((bf16[1024,1024]{0,1:T(8,128)(2,1)}), bf16[256,1024]{0,1:T(8,128)(2,1)}) %reduce-scatter.3.cloned.1.call-update) | async-done | bytes 524304 | tf_op jit(solution)/shard_map/reduce_scatter | solution.py:712
  351.4 3.9 fusion.94
  355.4 81.9 %combine_rows.1 = bf16[8,64,1024]{2,1,0:T(8,128)(2,1)} custom-call(bf16[8,4,64,1024]{3,2,1,0:T(8,128)(2,1)} %get-tuple-element.163.part_in, bf16[1,1024]{1,0:T(2,128)(2,1)} %bias_ref.1), custom_call_target="tpu_custom_call" | custom-call | tf_op jit(solution)/shard_map/combine_rows/pallas_call | solution.py:370
  447.3 39.3 %all-reduce = (f32[1024]{0:T(1024)}, f32[1024]{0:T(1024)}, f32[1024]{0:T(1024)}, f32[1024]{0:T(1024)}, f32[1024]{0:T(1024)}, /*index=5*/f32[1024]{0:T(1024)}, f32[1024]{0:T(1024)}) all-reduce(f32[1024]{0:T(1024)S(1)} %get-tuple-element.343, f32[1024]{0:T(1024)S(1)} %get-tuple-element.346, ...), channel_id=1, replica_groups=mesh['seq'=4,'exp'=8] {'seq','exp'}, use_global_device_ids=true, to_apply=%region_25.26 | all-reduce | flops 7168 | bytes 57344 | tf_op jit(solution)/shard_map/psum | solution.py:751
  489.5 176.6 %all-reduce.4.cloned.1.call-done = (f32[1024,1024]{1,0:T(8,128)}, f32[1024,1024]{1,0:T(8,128)}, f32[1024,1024]{1,0:T(8,128)}, f32[1024,1024]{1,0:T(8,128)}) async-done(((f32[1024,1024]{1,0:T(8,128)}, f32[1024,1024]{1,0:T(8,128)}, f32[1024,1024]{1,0:T(8,128)}, f32[1024,1024]{1,0:T(8,128)}), (f32[1024,1024]{1,0:T(8,128)}, f32[1024,1024]{1,0:T(8,128)}, f32[1024,1024]{1,0:T(8,128)}, ...) | async-done | bytes 16777232 | tf_op jit(solution)/shard_map/psum | solution.py:751
  666.0 4.9 copy.119
  (243 shorter events, 102.1 us)
Async XLA Ops:
  7.2 7.7 %copy-start = (bf16[1024,1024]{1,0:T(8,128)(2,1)S(1)}, bf16[1024,1024]{1,0:T(8,128)(2,1)}, u32[]{:S(2)}) copy-start(bf16[1024,1024]{1,0:T(8,128)(2,1)} %param.31) | copy-start | bytes 6291460
  7.2 7.7 %copy-start.5 = (bf16[1,256,1024]{2,1,0:T(8,128)(2,1)S(1)}, bf16[1,256,1024]{2,1,0:T(8,128)(2,1)}, u32[]{:S(2)}) copy-start(bf16[1,256,1024]{2,1,0:T(8,128)(2,1)} %param.23) | copy-start | bytes 1572868
  7.2 7.6 %copy-start.46 = (bf16[1024]{0:T(1024)(128)(2,1)S(1)}, bf16[1024]{0:T(1024)(128)(2,1)}, u32[]{:S(2)}) copy-start(bf16[1024]{0:T(1024)(128)(2,1)} %param.32) | copy-start | bytes 6148
  7.2 74.6 %all-gather.3.cloned.1.call-start = ((), (), s32[]{:S(2)}) async-start(), calls=%async_computation.2 | async-start | bytes 2621440 | tf_op jit(solution)/shard_map/all_gather | solution.py:584
  8.6 9.1 %copy-start.38 = (f32[256]{0:T(256)}, f32[256]{0:T(256)S(1)}, u32[]{:S(2)}) copy-start(f32[256]{0:T(256)S(1)} %broadcast_multiply_fusion.1) | copy-start | bytes 3076
  10.0 6.5 copy-start.42
  10.0 7.7 %copy-start.40 = (f32[256]{0:T(256)}, f32[256]{0:T(256)S(1)}, u32[]{:S(2)}) copy-start(f32[256]{0:T(256)S(1)} %fusion.90) | copy-start | bytes 3076
  10.7 7.0 %copy-start.34 = (f32[1024]{0:T(1024)}, f32[1024]{0:T(1024)S(1)}, u32[]{:S(2)}) copy-start(f32[1024]{0:T(1024)S(1)} %convert_element_type.145) | copy-start | bytes 12292
  11.4 6.4 copy-start.36
  11.4 5.4 copy-start.47
  11.4 5.4 copy-start.48
  11.4 5.4 copy-start.49
  11.4 5.4 copy-start.50
  11.4 5.4 copy-start.44
  14.8 90.3 %all-gather.5.cloned.1.call-start = ((), (), s32[]{:S(2)}) async-start(), calls=%async_computation.3 | async-start | bytes 2621440 | tf_op jit(solution)/shard_map/all_gather | solution.py:585
  16.5 296.0 %reduce-scatter.5.cloned.1.call-start = ((), (), s32[]{:S(2)}) async-start(), calls=%async_computation.5 | async-start | bytes 2621440 | tf_op jit(solution)/shard_map/reduce_scatter | solution.py:718
  142.6 89.7 %copy-start.8 = (f32[256,1024]{1,0:T(8,128)S(1)}, f32[256,1024]{1,0:T(8,128)}, u32[]{:S(2)}) copy-start(f32[256,1024]{1,0:T(8,128)} %copy-done.7) | copy-start | bytes 3145732
  275.0 76.3 %reduce-scatter.3.cloned.1.call-start = ((), (), s32[]{:S(2)}) async-start(), calls=%async_computation.4 | async-start | bytes 2621440 | tf_op jit(solution)/shard_map/reduce_scatter | solution.py:712
  280.8 385.3 %all-reduce.4.cloned.1.call-start = ((), (), s32[]{:S(2)}) async-start(), calls=%async_computation.6 | async-start | bytes 33554432 | tf_op jit(solution)/shard_map/psum | solution.py:751
  355.3 86.2 %copy-start.14 = (bf16[256,16,64]{0,2,1:T(8,128)(2,1)S(1)}, bf16[256,16,64]{0,2,1:T(8,128)(2,1)}, u32[]{:S(2)}) copy-start(bf16[256,16,64]{0,2,1:T(8,128)(2,1)} %copy-done.13) | copy-start | bytes 1572868
  437.3 6.6 copy-start.26
  437.3 6.8 copy-start.24
  437.3 6.8 copy-start.27
  444.9 41.7 %copy-start.16 = (bf16[1,256,1024]{2,1,0:T(8,128)(2,1)S(1)}, bf16[1,256,1024]{2,1,0:T(8,128)(2,1)}, u32[]{:S(2)}) copy-start(bf16[1,256,1024]{2,1,0:T(8,128)(2,1)} %param.41) | copy-start | bytes 1572868
  (44 other events, 115.8 us)
Sparse Core Ops, SparseCore 0:
  14.9 52.3 all-gather.2
  69.8 35.3 all-gather.4
  275.2 37.2 reduce-scatter.4
  316.1 35.1 reduce-scatter.2
  358.8 307.2 all-reduce.3

commit v2 on v1

--- a/solution.py
+++ b/solution.py
@@ -7,36 +7,6 @@
 from jax.experimental import pallas as pl
 from jax.experimental.pallas import tpu as pltpu
 from jax.sharding import PartitionSpec as P
-
-
-HEADS = 16
-HEAD_DIM = 64
-
-
-EPSILON = 1e-05
-SCORE_SCALE = 0.125
-MASKED_SCORE = -1e30
-
-
-def norm_layer(values_in, gain_vec, shift_vec):
-    center = values_in - jnp.mean(values_in, axis=-1, keepdims=True)
-    inv_std = lax.rsqrt(jnp.mean(center * center, axis=-1, keepdims=True) + EPSILON)
-    return center * inv_std * gain_vec + shift_vec
-
-
-def segment_ids(positions, seq_ends):
-    return jnp.sum((positions[:, None] >= seq_ends[None, :]).astype(jnp.int32), axis=1)
-
-
-def visible_pairs(query_pos, query_seg, key_pos, key_seg):
-    return ((query_seg[:, None] == key_seg[None, :]) & (key_pos[None, :] <= query_pos[:, None]))[
-        None
-    ]
-
-
-def project(left_op, right_op):
-    return jnp.dot(left_op, right_op, preferred_element_type=jnp.float32)
-
 
 MESH = pl.DeviceIdType.MESH
 F32 = jnp.float32
@@ -69,24 +39,20 @@
         chip = lax.rem(self.chip + way * hop + chips, chips)
         return chip * 2 + lax.rem(self.core + step, 2)
 
-    def greet(self, seq=True, exp=True):
+    def greet(self, diag=False):
         barrier = pltpu.get_barrier_semaphore()
-        count = 0
-        if seq:
-            for other in (self.near, self.far):
-                pl.semaphore_signal(barrier, inc=1, device_id=(other, self.e), device_id_type=MESH)
-            count += 2
-        if exp:
-
-            def tell(step, carry):
-                pl.semaphore_signal(
-                    barrier, inc=1, device_id=(self.s, self.peer(step, 1)), device_id_type=MESH
-                )
-                return carry
-
-            lax.fori_loop(1, self.n_exp, tell, 0)
-            count += self.n_exp - 1
-        pl.semaphore_wait(barrier, count)
+        others = (self.near, self.far, self.diag) if diag else (self.near, self.far)
+        for other in others:
+            pl.semaphore_signal(barrier, inc=1, device_id=(other, self.e), device_id_type=MESH)
+
+        def tell(step, carry):
+            pl.semaphore_signal(
+                barrier, inc=1, device_id=(self.s, self.peer(step, 1)), device_id_type=MESH
+            )
+            return carry
+
+        lax.fori_loop(1, self.n_exp, tell, 0)
+        pl.semaphore_wait(barrier, len(others) + self.n_exp - 1)
 
     def to_seq(self, src, dst, send_sem, recv_sem, other):
         return pltpu.make_async_remote_copy(
@@ -186,8 +152,7 @@
         self.total, self.back, self.slots = total, back, slots
         self.seq_send, self.seq_recv = seq_sems
         self.exp_send, self.exp_recv = exp_sems
-        self.cap = back.shape[1]
-        self.half = self.cap // 2
+        self.half = part.shape[2] // 2
 
     @staticmethod
     def scratch(n_exp, cap, width):
@@ -251,24 +216,29 @@
             self.total.at[step], self.back.at[p.e], self.exp_send.at[step], self.exp_recv.at[step], other
         )
 
-    def finish(self, step, bias=None):
-        p = self.place
-        slot = self._slot(step)
+    def arrived(self, step):
         copies = self.copies(step)
         for c in copies[2:]:
             c.wait_recv()
+        for c in copies:
+            c.wait_send()
+
+    def summed(self, step, half):
+        rows = pl.ds(half * self.half, self.half)
+        return (
+            self.part[self._slot(step), self.place.s, rows].astype(F32)
+            + self.landing[step, half].astype(F32)
+            + self.landing[step, 2 + half].astype(F32)
+        )
+
+    def finish(self, step, bias=None):
+        p = self.place
+        self.arrived(step)
         for half in range(2):
-            rows = pl.ds(half * self.half, self.half)
-            value = (
-                self.part[slot, p.s, rows].astype(F32)
-                + self.landing[step, half].astype(F32)
-                + self.landing[step, 2 + half].astype(F32)
-            )
+            value = self.summed(step, half)
             if bias is not None:
                 value = value + bias
-            self.total[step, rows] = value.astype(BF16)
-        for c in copies:
-            c.wait_send()
+            self.total[step, pl.ds(half * self.half, self.half)] = value.astype(BF16)
 
         @pl.when(step > 0)
         def _():
@@ -288,100 +258,6 @@
             return carry
 
         lax.fori_loop(1, p.n_exp, body, 0)
-
-
-def dispatch_rows(send, collective_id):
-    n_exp, cap, width = send.shape
-
-    def kernel(send, held, *sems):
-        p = Place(n_exp)
-        p.greet()
-        d = Dispatch(p, send, held, sems[0:2], sems[2:4])
-        d.own()
-
-        d.start_seq(0)
-        for step in range(1, n_exp):
-            d.start_exp(step)
-
-        def loop(t, carry):
-            @pl.when(t < n_exp)
-            def _():
-                d.start_seq(t)
-
-            d.relay(t - 1)
-
-            @pl.when(t >= 2)
-            def _():
-                d.arrived(t - 2)
-
-            return carry
-
-        lax.fori_loop(1, n_exp + 1, loop, 0)
-        d.arrived(n_exp - 1)
-        d.drain()
-
-    return pl.pallas_call(
-        kernel,
-        out_shape=jax.ShapeDtypeStruct((n_exp, 4, cap, width), BF16),
-        in_specs=[pl.BlockSpec(memory_space=pltpu.VMEM)],
-        out_specs=pl.BlockSpec(memory_space=pltpu.VMEM),
-        scratch_shapes=Dispatch.scratch(n_exp),
-        compiler_params=pltpu.CompilerParams(
-            collective_id=collective_id, has_side_effects=True, vmem_limit_bytes=VMEM_LIMIT
-        ),
-        name="dispatch_rows",
-    )(send)
-
-
-def combine_rows(part, bias, collective_id):
-    n_exp, _, cap, width = part.shape
-
-    def kernel(part_in, bias_ref, back, part, load_sem, passing, landing, total, *sems):
-        p = Place(n_exp)
-
-        def load(step):
-            return pltpu.make_async_copy(part_in.at[step], part.at[step], load_sem.at[step])
-
-        for step in range(n_exp):
-            load(step).start()
-        p.greet()
-        c = Combine(p, part, passing, landing, total, back, sems[0:2], sems[2:4], n_exp)
-        bias_row = bias_ref[...].astype(F32)
-
-        def loop(t, carry):
-            @pl.when(t < n_exp)
-            def _():
-                load(t).wait()
-                c.start(t)
-
-            @pl.when((t >= 2) & (t < n_exp + 2))
-            def _():
-                c.pass_on(t - 2)
-
-            @pl.when(t >= 4)
-            def _():
-                c.finish(t - 4, bias_row)
-
-            return carry
-
-        lax.fori_loop(0, n_exp + 4, loop, 0)
-        c.drain()
-
-    return pl.pallas_call(
-        kernel,
-        out_shape=jax.ShapeDtypeStruct((n_exp, cap, width), BF16),
-        in_specs=[pl.BlockSpec(memory_space=pl.ANY), pl.BlockSpec(memory_space=pltpu.VMEM)],
-        out_specs=pl.BlockSpec(memory_space=pltpu.VMEM),
-        scratch_shapes=[
-            pltpu.VMEM((n_exp, 4, cap, width), BF16),
-            pltpu.SemaphoreType.DMA((n_exp,)),
-        ]
-        + Combine.scratch(n_exp, cap, width),
-        compiler_params=pltpu.CompilerParams(
-            collective_id=collective_id, has_side_effects=True, vmem_limit_bytes=VMEM_LIMIT
-        ),
-        name="combine_rows",
-    )(part, bias)
 
 
 GELU_A = math.sqrt(2.0 / math.pi)
@@ -533,7 +409,804 @@
     )(send, cot_rows, w_up, b_up, w_down)
 
 
+EPSILON = 1e-05
+SCORE_SCALE = 0.125
+MASKED_SCORE = -1e30
+HEAD_DIM = 64
+HEADS = 16
+
+
+class Gather:
+    def __init__(self, place, held, send_sems, recv_sems):
+        self.place, self.held = place, held
+        self.send_sems, self.recv_sems = send_sems, recv_sems
+        self.half = held.shape[1] // 2
+
+    @staticmethod
+    def scratch():
+        return [pltpu.SemaphoreType.DMA((6,)), pltpu.SemaphoreType.DMA((6,))]
+
+    def copies(self, lanes=range(6)):
+        p = self.place
+        spec = (
+            (p.s, 0, p.near),
+            (p.s, 1, p.far),
+            (p.s, 1, p.near),
+            (p.s, 0, p.far),
+            (p.near, 0, p.far),
+            (p.far, 1, p.near),
+        )
+        made = []
+        for n in lanes:
+            owner, half, other = spec[n]
+            part = self.held.at[owner, pl.ds(half * self.half, self.half)]
+            made.append(p.to_seq(part, part, self.send_sems.at[n], self.recv_sems.at[n], other))
+        return made
+
+    def start(self):
+        for c in self.copies(range(4)):
+            c.start()
+
+    def relay(self):
+        for c, out in zip(self.copies((0, 1)), self.copies((4, 5))):
+            c.wait_recv()
+            out.start()
+
+    def wait(self, lanes):
+        for c in self.copies(lanes):
+            c.wait_recv()
+
+    def drain(self):
+        for c in self.copies():
+            c.wait_send()
+
+
+def layer_norm(values, gain, shift):
+    center = values - jnp.mean(values, axis=-1, keepdims=True)
+    inv_std = lax.rsqrt(jnp.mean(center * center, axis=-1, keepdims=True) + EPSILON)
+    xhat = center * inv_std
+    return xhat * gain + shift, xhat, inv_std
+
+
+def norm_back(grad, xhat, inv_std, gain):
+    d = grad * gain
+    return (
+        d - jnp.mean(d, axis=-1, keepdims=True) - xhat * jnp.mean(d * xhat, axis=-1, keepdims=True)
+    ) * inv_std
+
+
+def row_choice(ids, n_exp, cap):
+    tokens = ids.shape[0]
+    named = (ids == lax.broadcasted_iota(jnp.int32, (tokens, 128), 1)).astype(BF16)
+    before = (
+        lax.broadcasted_iota(jnp.int32, (tokens, tokens), 1)
+        < lax.broadcasted_iota(jnp.int32, (tokens, tokens), 0)
+    ).astype(BF16)
+    earlier = dot(before, named) * named.astype(F32)
+    slot = jnp.sum(earlier, axis=1, keepdims=True).astype(jnp.int32) + ids * cap
+    return (slot == lax.broadcasted_iota(jnp.int32, (tokens, n_exp * cap), 1)).astype(BF16)
+
+
+def segment_of(position, lengths):
+    end = jnp.int32(0)
+    count = jnp.zeros_like(position)
+    for n in range(lengths.shape[1]):
+        end = end + lengths[0, n]
+        count = count + (position >= end).astype(jnp.int32)
+    return count
+
+
+def head_mask(rows, width, head):
+    lane = lax.broadcasted_iota(jnp.int32, (rows, width), 1)
+    return (lane >= head * HEAD_DIM) & (lane < (head + 1) * HEAD_DIM)
+
+
+def front_part(
+    tokens, lengths, ids, ln1, w_qkv, b_qkv, w_out, b_out, ln2, cotangent, n_exp, collective_id
+):
+    tok, width = tokens.shape
+    n_seq = 4
+    total = n_seq * tok
+    cols = width // n_seq
+    heads = cols // HEAD_DIM
+    cap = 2 * tok // n_exp
+    q_block = 256
+
+    def kernel(tok_ref, len_ref, ids_ref, ln1_ref, wq_in, wk_in, wv_in, bqkv_ref, wo_in, bo_ref, ln2_ref, cot_ref,
+               n1_ref, q_ref, k_ref, v_ref, attn_ref, lse_ref, resid_ref, pick_ref, sendn_ref, cotall_ref,
+               xall, w_qkv, w_o, sendc, attn_out, attn_in, local_sems, a2a_send, a2a_recv, *rest):
+        p = Place(n_exp)
+        mine = pl.ds(pl.multiple_of(p.s * cols, cols), cols)
+        loads = [
+            pltpu.make_async_copy(src.at[:, mine], w_qkv.at[:, pl.ds(n * cols, cols)], local_sems.at[n])
+            for n, src in enumerate((wq_in, wk_in, wv_in))
+        ]
+        load_out = pltpu.make_async_copy(wo_in, w_o, local_sems.at[3])
+        for c in loads:
+            c.start()
+        load_out.start()
+        xall[p.s] = tok_ref[...]
+        p.greet(diag=True)
+        gather = Gather(p, xall, rest[0], rest[1])
+        gather.start()
+        pick = row_choice(ids_ref[...], n_exp, cap)
+        pick_ref[...] = pick
+        sendc[...] = dot(pick, cot_ref[...], ((0,), (0,))).astype(BF16).reshape(n_exp, cap, width)
+        d = Dispatch(p, sendc, cotall_ref, rest[2:4], rest[4:6])
+        for step in range(1, n_exp):
+            d.start_exp(step)
+        d.own()
+        gain1 = ln1_ref[0:1, :].astype(F32)
+        bias1 = ln1_ref[1:2, :].astype(F32)
+        bq = bqkv_ref[0:1, mine].astype(F32)
+        bv = bqkv_ref[1:2, mine].astype(F32)
+
+        def project(owner):
+            x = xall[owner].astype(F32)
+            normed = layer_norm(x, gain1, bias1)[0].astype(BF16)
+            rows = pl.ds(pl.multiple_of(owner * tok, tok), tok)
+            n1_ref[rows, :] = normed
+            out = dot(normed, w_qkv[...])
+            q = (out[:, 0:cols] + bq).astype(BF16)
+            q_ref[rows, :] = (q.astype(F32) * SCORE_SCALE).astype(BF16)
+            k_ref[rows, :] = out[:, cols : 2 * cols].astype(BF16)
+            v_ref[rows, :] = (out[:, 2 * cols :] + bv).astype(BF16)
+
+        for c in loads:
+            c.wait()
+        project(p.s)
+        gather.relay()
+        gather.wait((2, 3))
+        project(p.near)
+        project(p.far)
+        gather.wait((4, 5))
+        d.start_seq(0)
+        project(p.diag)
+
+        background = []
+        for t in range(1, n_exp + 2):
+            def some(t=t):
+                if t < n_exp:
+                    d.start_seq(t)
+                if t <= n_exp:
+                    d.relay(t - 1)
+                if t >= 2:
+                    d.arrived(t - 2)
+            background.append(some)
+
+        def a2a(owner):
+            return p.to_seq(
+                attn_out.at[owner], attn_in.at[p.s], a2a_send.at[owner], a2a_recv.at[p.s], owner
+            )
+
+        def a2a_from(owner):
+            return p.to_seq(
+                attn_out.at[owner], attn_in.at[owner], a2a_send.at[owner], a2a_recv.at[owner], owner
+            )
+
+        for n in reversed(range(total // q_block)):
+            seen = (n + 1) * q_block
+            rows = pl.ds(n * q_block, q_block)
+            q_pos = lax.broadcasted_iota(jnp.int32, (q_block, 1), 0) + n * q_block
+            k_pos = lax.broadcasted_iota(jnp.int32, (1, seen), 1)
+            allowed = (segment_of(q_pos, len_ref) == segment_of(k_pos, len_ref)) & (k_pos <= q_pos)
+            q_rows = q_ref[rows, :]
+            acc = jnp.zeros((q_block, cols), F32)
+            lse = jnp.zeros((q_block, 128), F32)
+            lane = lax.broadcasted_iota(jnp.int32, (q_block, 128), 1)
+            for head in range(heads):
+                own = head_mask(q_block, cols, head)
+                scores = dot(jnp.where(own, q_rows, jnp.zeros_like(q_rows)), k_ref[0:seen, :], ((1,), (1,)))
+                scores = jnp.where(allowed, scores, MASKED_SCORE)
+                top = jnp.max(scores, axis=1, keepdims=True)
+                weights = jnp.exp(scores - top)
+                sums = jnp.sum(weights, axis=1, keepdims=True)
+                out = dot(weights.astype(BF16), v_ref[0:seen, :]) / sums
+                acc = jnp.where(own, out, acc)
+                lse = jnp.where(lane == head, top + jnp.log(sums), lse)
+            attn_ref[rows, :] = acc
+            lse_ref[:, rows] = jnp.transpose(lse)[0:8, :]
+            owner, at = (n * q_block) // tok, (n * q_block) % tok
+            attn_out[owner, pl.ds(at, q_block)] = acc.astype(BF16)
+            if at == 0:
+
+                @pl.when(p.s != owner)
+                def _(owner=owner):
+                    a2a(owner).start()
+
+                @pl.when(p.s == owner)
+                def _(owner=owner):
+                    attn_in[owner] = attn_out[owner]
+
+            if background and n % 2 == 1:
+                background.pop(0)()
+        load_out.wait()
+        sums = tok_ref[...].astype(F32) + bo_ref[...].astype(F32)
+        for owner in range(n_seq):
+
+            @pl.when(p.s != owner)
+            def _(owner=owner):
+                a2a_from(owner).wait_recv()
+
+            sums = sums + dot(attn_in[owner], w_o[pl.ds(owner * cols, cols), :])
+        resid_ref[...] = sums
+        normed_two = layer_norm(sums, ln2_ref[0:1, :].astype(F32), ln2_ref[1:2, :].astype(F32))[0].astype(BF16)
+        sendn_ref[...] = dot(pick_ref[...], normed_two, ((0,), (0,))).astype(BF16).reshape(n_exp, cap, width)
+        while background:
+            background.pop(0)()
+        for owner in range(n_seq):
+
+            @pl.when(p.s != owner)
+            def _(owner=owner):
+                a2a(owner).wait_send()
+
+        gather.drain()
+        d.drain()
+
+    vmem = pl.BlockSpec(memory_space=pltpu.VMEM)
+    hbm = pl.BlockSpec(memory_space=pl.ANY)
+    smem = pl.BlockSpec(memory_space=pltpu.SMEM)
+    shape = jax.ShapeDtypeStruct
+    return pl.pallas_call(
+        kernel,
+        out_shape=[
+            shape((total, width), BF16),
+            shape((total, cols), BF16),
+            shape((total, cols), BF16),
+            shape((total, cols), BF16),
+            shape((total, cols), F32),
+            shape((8, total), F32),
+            shape((tok, width), F32),
+            shape((tok, n_exp * cap), BF16),
+            shape((n_exp, cap, width), BF16),
+            shape((n_exp, n_seq, cap, width), BF16),
+        ],
+        in_specs=[vmem, smem, vmem, vmem, hbm, hbm, hbm, vmem, hbm, vmem, vmem, vmem],
+        out_specs=[vmem] * 10,
+        scratch_shapes=[
+            pltpu.VMEM((n_seq, tok, width), BF16),
+            pltpu.VMEM((width, 3 * cols), BF16),
+            pltpu.VMEM((width, width), BF16),
+            pltpu.VMEM((n_exp, cap, width), BF16),
+            pltpu.VMEM((n_seq, tok, cols), BF16),
+            pltpu.VMEM((n_seq, tok, cols), BF16),
+            pltpu.SemaphoreType.DMA((4,)),
+            pltpu.SemaphoreType.DMA((n_seq,)),
+            pltpu.SemaphoreType.DMA((n_seq,)),
+        ]
+        + Gather.scratch()
+        + Dispatch.scratch(n_exp),
+        compiler_params=pltpu.CompilerParams(
+            collective_id=collective_id, has_side_effects=True, vmem_limit_bytes=VMEM_LIMIT
+        ),
+        name="front_part",
+    )(tokens, lengths, ids, ln1, *w_qkv, b_qkv, w_out, b_out, ln2, cotangent)
+
+
+class SumAll:
+    def __init__(self, place, src, core_in, mine, chip_in, res, result, local_sem, sems, by_rows):
+        self.place, self.src, self.core_in, self.mine = place, src, core_in, mine
+        self.chip_in, self.res, self.result, self.local_sem = chip_in, res, result, local_sem
+        (self.core_sems, self.rs_send, self.rs_recv, self.ag_send, self.ag_recv,
+         self.seq_send, self.seq_recv, self.pair_send, self.pair_recv) = sems
+        self.chips = place.n_exp // 2
+        self.by_rows = by_rows
+        p = place
+        self.sibling = p.chip * 2 + (1 - p.core)
+
+    @staticmethod
+    def scratch(n_exp, rows, width):
+        chips = n_exp // 2
+        dma = pltpu.SemaphoreType.DMA
+        return [
+            pltpu.VMEM((2, chips, rows, width), BF16),
+            pltpu.VMEM((chips, rows, width), BF16),
+            pltpu.VMEM((chips, rows, width), BF16),
+            pltpu.VMEM((chips, rows, width), BF16),
+            pltpu.VMEM((rows, width), BF16),
+            dma((1,)),
+            dma((2,)),
+            dma((chips,)),
+            dma((chips,)),
+            dma((chips,)),
+            dma((chips,)),
+            dma((chips, 6)),
+            dma((chips, 6)),
+            dma((chips, 4)),
+            dma((chips, 4)),
+        ]
+
+    def chip(self, hop):
+        return lax.rem(self.place.chip + hop, self.chips)
+
+    def exp(self, hop):
+        return self.chip(hop) * 2 + self.place.core
+
+    def _core(self):
+        p = self.place
+        return p.to_exp(
+            self.src.at[1 - p.core], self.core_in, self.core_sems.at[0], self.core_sems.at[1], self.sibling
+        )
+
+    def start(self):
+        self._core().start()
+
+    def _spread(self, hop):
+        p = self.place
+        to = self.chip(hop)
+        return p.to_exp(
+            self.mine.at[to], self.chip_in.at[p.chip], self.rs_send.at[to], self.rs_recv.at[p.chip], self.exp(hop)
+        )
+
+    def _spread_from(self, hop):
+        p = self.place
+        at = self.chip(hop)
+        return p.to_exp(
+            self.mine.at[at], self.chip_in.at[at], self.rs_send.at[at], self.rs_recv.at[at], self.exp(hop)
+        )
+
+    def spread(self):
+        p = self.place
+        self._core().wait_recv()
+        for n in range(self.chips):
+            self.mine[n] = (self.src[p.core, n].astype(F32) + self.core_in[n].astype(F32)).astype(BF16)
+        for hop in range(1, self.chips):
+            self._spread(hop).start()
+
+    def _local(self):
+        p = self.place
+        return pltpu.make_async_copy(self.res, self.result.at[p.s, p.e], self.local_sem.at[0])
+
+    def _share(self, hop):
+        p = self.place
+        to = self.chip(hop)
+        return p.to_exp(
+            self.res, self.result.at[p.s, p.e], self.ag_send.at[to], self.ag_recv.at[p.chip], self.exp(hop)
+        )
+
+    def _share_from(self, hop):
+        p = self.place
+        at = self.chip(hop)
+        return p.to_exp(
+            self.res, self.result.at[p.s, self.exp(hop)], self.ag_send.at[at], self.ag_recv.at[at], self.exp(hop)
+        )
+
+    def _part(self, hop, owner, half):
+        where = self.result.at[owner, self.exp(hop)]
+        rows, width = where.shape
+        if self.by_rows:
+            return where.at[pl.ds(half * (rows // 2), rows // 2)]
+        return where.at[:, pl.ds(half * (width // 2), width // 2)]
+
+    def copies(self, hop, lanes=range(6)):
+        p = self.place
+        spec = (
+            (p.s, 0, p.near),
+            (p.s, 1, p.far),
+            (p.s, 1, p.near),
+            (p.s, 0, p.far),
+            (p.near, 0, p.far),
+            (p.far, 1, p.near),
+        )
+        made = []
+        for n in lanes:
+            owner, half, other = spec[n]
+            part = self._part(hop, owner, half)
+            made.append(p.to_seq(part, part, self.seq_send.at[hop, n], self.seq_recv.at[hop, n], other))
+        return made
+
+    def _pair(self, hop, n):
+        p = self.place
+        part = self.result.at[(p.s, p.near, p.far, p.diag)[n], self.exp(hop)]
+        return p.to_exp(part, part, self.pair_send.at[hop, n], self.pair_recv.at[hop, n], self.sibling)
+
+    def _pair_from(self, hop, n):
+        p = self.place
+        owner = (p.s, p.near, p.far, p.diag)[n]
+        part = self.result.at[owner, self.chip(hop) * 2 + (1 - p.core)]
+        return p.to_exp(part, part, self.pair_send.at[hop, n], self.pair_recv.at[hop, n], self.sibling)
+
+    def reduce(self):
+        p = self.place
+        for hop in range(1, self.chips):
+            self._spread_from(hop).wait_recv()
+        total = self.mine[p.chip].astype(F32)
+        for hop in range(1, self.chips):
+            total = total + self.chip_in[self.chip(hop)].astype(F32)
+        self.res[...] = total.astype(BF16)
+        self._local().start()
+        for hop in range(1, self.chips):
+            self._share(hop).start()
+        self._local().wait()
+
+    def forward(self, hop):
+        if hop > 0:
+            self._share_from(hop).wait_recv()
+        for c in self.copies(hop, range(4)):
+            c.start()
+        self._pair(hop, 0).start()
+
+    def relay(self, hop):
+        for c, out in zip(self.copies(hop, (0, 1)), self.copies(hop, (4, 5))):
+            c.wait_recv()
+            out.start()
+
+    def arrived(self, hop):
+        for c in self.copies(hop, (2, 3)):
+            c.wait_recv()
+        self._pair(hop, 1).start()
+        self._pair(hop, 2).start()
+        for c in self.copies(hop, (4, 5)):
+            c.wait_recv()
+        self._pair(hop, 3).start()
+
+    def drain(self):
+        self._core().wait_send()
+        for hop in range(1, self.chips):
+            self._spread(hop).wait_send()
+            self._share(hop).wait_send()
+        for hop in range(self.chips):
+            for c in self.copies(hop):
+                c.wait_send()
+            for n in range(4):
+                self._pair(hop, n).wait_send()
+                self._pair_from(hop, n).wait_recv()
+
+
+def back_part(
+    grad_back, pick, resid, ln2, cotangent, w_out, q, k, v, attn, lse, n1, w_qkv, tokens, ln1, ffn_part, b_down,
+    lengths, collective_id
+):
+    tok, width = tokens.shape
+    n_exp, n_seq, cap, _ = ffn_part.shape
+    total = n_seq * tok
+    cols = width // n_seq
+    heads = cols // HEAD_DIM
+    q_block = 256
+    rows_w, rows_o = width // n_exp, cols // n_exp
+    n_sum = len(SumAll.scratch(n_exp, 16, 128))
+    n_comb = len(Combine.scratch(n_exp, cap, width))
+
+    def kernel(gback_ref, pick_ref, resid_ref, ln2_ref, cot_ref, wo_in, q_ref, k_ref, v_ref, attn_ref, lse_ref,
+               n1_in, wq_in, wk_in, wv_in, tok_ref, ln1_ref, ffn_in, bd_ref, len_ref,
+               out_ref, gin_ref, vec_ref, gw_ref, go_ref,
+               gout, gattn, dqkv, dk, dv, n1, w_all, w_o, part, red_part, ret, vec_own, vec_seq, vec_exp,
+               local_sems, load_sems, vs_send, vs_recv, ve_send, ve_recv, *rest):
+        p = Place(n_exp)
+        mine = pl.ds(pl.multiple_of(p.s * cols, cols), cols)
+        load_o = pltpu.make_async_copy(wo_in.at[mine, :], w_o, local_sems.at[3])
+        loads = [
+            pltpu.make_async_copy(src.at[:, mine], w_all.at[:, pl.ds(n * cols, cols)], local_sems.at[n])
+            for n, src in enumerate((wq_in, wk_in, wv_in))
+        ] + [pltpu.make_async_copy(n1_in, n1, local_sems.at[4])]
+        load_o.start()
+        for c in loads:
+            c.start()
+
+        def load(step):
+            return pltpu.make_async_copy(ffn_in.at[step], part.at[step], load_sems.at[step])
+
+        for step in range(n_exp):
+            load(step).start()
+        p.greet(diag=True)
+        at = 0
+        gather = Gather(p, gout, rest[0], rest[1])
+        at = 2
+        comb = Combine(p, part, *rest[at : at + 3], ret, rest[at + 3 : at + 5], rest[at + 5 : at + 7], n_exp)
+        at += n_comb
+        red = Combine(p, red_part, rest[at], rest[at + 1], None, None, rest[at + 2 : at + 4], (None, None), 1)
+        at += 4
+        sum_o = SumAll(p, *rest[at : at + 5], go_ref, rest[at + 5], rest[at + 6 : at + n_sum], False)
+        at += n_sum
+        sum_w = SumAll(p, *rest[at : at + 5], gw_ref, rest[at + 5], rest[at + 6 : at + n_sum], True)
+        src_o, src_w = sum_o.src, sum_w.src
+
+        g_two = dot(pick_ref[...], gback_ref[...].reshape(n_exp * cap, width))
+        gain2 = ln2_ref[0:1, :].astype(F32)
+        _, xhat, inv_std = layer_norm(resid_ref[...], gain2, 0.0)
+        g_resid = cot_ref[...].astype(F32) + norm_back(g_two, xhat, inv_std, gain2)
+        gin_ref[...] = g_resid
+        g_low = g_resid.astype(BF16)
+        gout[p.s] = g_low
+        gather.start()
+        vec_own[...] = jnp.zeros_like(vec_own)
+        vec_own[4:5, :] = jnp.sum(g_low.astype(F32), axis=0, keepdims=True)
+        vec_own[5:6, :] = jnp.sum(g_two * xhat, axis=0, keepdims=True)
+        vec_own[6:7, :] = jnp.sum(g_two, axis=0, keepdims=True)
+        load_o.wait()
+
+        def grad_attn(owner):
+            rows = pl.ds(pl.multiple_of(owner * tok, tok), tok)
+            gattn[rows, :] = dot(gout[owner], w_o[...], ((1,), (1,))).astype(BF16)
+
+        grad_attn(p.s)
+        dk[...] = jnp.zeros_like(dk)
+        dv[...] = jnp.zeros_like(dv)
+        gather.relay()
+        gather.wait((2, 3))
+        grad_attn(p.near)
+        grad_attn(p.far)
+        gather.wait((4, 5))
+        grad_attn(p.diag)
+
+        g_all = gout[...].reshape(total, width)
+        for b in range(cols // 128):
+            a_low = attn_ref[:, b * 128 : (b + 1) * 128].astype(BF16)
+            got = dot(a_low, g_all, ((0,), (0,))).astype(BF16)
+            for n in range(128 // rows_o):
+                e = b * (128 // rows_o) + n
+                src_o[e % 2, e // 2] = got[n * rows_o : (n + 1) * rows_o]
+        sum_o.start()
+
+        bias_row = bd_ref[...].astype(F32)
+        background = []
+        for t in range(n_exp + 3):
+
+            def some(t=t):
+                if t < n_exp:
+                    load(t).wait()
+                    comb.start(t)
+                if 2 <= t < n_exp + 2:
+                    comb.pass_on(t - 2)
+                if t >= 3:
+                    comb.finish(t - 3, bias_row)
+
+            background.append(some)
+
+        def turn(count=1):
+            for _ in range(count):
+                if background:
+                    background.pop(0)()
+
+        blocks = total // q_block
+        head_rows = lax.broadcasted_iota(jnp.int32, (8, cols), 0)
+        head_lane = lax.broadcasted_iota(jnp.int32, (8, cols), 1)
+        per_head = (lax.div(head_lane, HEAD_DIM) == head_rows).astype(F32)
+        for n in reversed(range(blocks)):
+            turn(1)
+            seen = (n + 1) * q_block
+            rows = pl.ds(n * q_block, q_block)
+            q_pos = lax.broadcasted_iota(jnp.int32, (1, q_block), 1) + n * q_block
+            k_pos = lax.broadcasted_iota(jnp.int32, (seen, 1), 0)
+            allowed = (segment_of(q_pos, len_ref) == segment_of(k_pos, len_ref)) & (k_pos <= q_pos)
+            q_rows, g_rows = q_ref[rows, :], gattn[rows, :]
+            delta = lax.dot_general(
+                per_head, g_rows.astype(F32) * attn_ref[rows, :], (((1,), (1,)), ((), ())),
+                precision=lax.Precision.HIGHEST, preferred_element_type=F32,
+            )
+            k_seen, v_seen = k_ref[0:seen, :], v_ref[0:seen, :]
+            dq = jnp.zeros((q_block, cols), F32)
+            dk_new = jnp.zeros((seen, cols), F32)
+            dv_new = jnp.zeros((seen, cols), F32)
+            for head in range(heads):
+                own = head_mask(q_block, cols, head)
+                q_own = jnp.where(own, q_rows, jnp.zeros_like(q_rows))
+                g_own = jnp.where(own, g_rows, jnp.zeros_like(g_rows))
+                scores = dot(k_seen, q_own, ((1,), (1,)))
+                probs = jnp.where(allowed, jnp.exp(scores - lse_ref[head : head + 1, rows]), 0.0)
+                g_probs = dot(v_seen, g_own, ((1,), (1,)))
+                g_scores = (probs * (g_probs - delta[head : head + 1, :])).astype(BF16)
+                dk_new = dk_new + dot(g_scores, q_own)
+                dv_new = dv_new + dot(probs.astype(BF16), g_own)
+                dq = jnp.where(own, dot(g_scores, k_seen, ((0,), (0,))), dq)
+            dqkv[rows, 0:cols] = (dq * SCORE_SCALE).astype(BF16)
+            dk[0:seen, :] += dk_new
+            dv[0:seen, :] += dv_new
+            if n == blocks - 2:
+                sum_o.spread()
+        sum_o.reduce()
+        sum_o.forward(0)
+        dqkv[:, cols : 2 * cols] = dk[...].astype(BF16)
+        dqkv[:, 2 * cols :] = dv[...].astype(BF16)
+        for c in loads:
+            c.wait()
+        d_all = dqkv[...]
+        for b in range(width // 128):
+            got = dot(n1[:, b * 128 : (b + 1) * 128], d_all, ((0,), (0,))).astype(BF16)
+            for n in range(128 // rows_w):
+                e = b * (128 // rows_w) + n
+                src_w[e % 2, e // 2] = got[n * rows_w : (n + 1) * rows_w]
+        sum_w.start()
+        for owner in range(n_seq):
+            piece = dqkv[pl.ds(owner * tok, tok), :]
+            red_part[0, owner] = dot(piece, w_all[...], ((1,), (1,))).astype(BF16)
+        red.start(0)
+        sum_w.spread()
+        vec_own[2:3, mine] = jnp.sum(dqkv[:, 0:cols].astype(F32), axis=0, keepdims=True)
+        vec_own[3:4, mine] = jnp.sum(dqkv[:, 2 * cols :].astype(F32), axis=0, keepdims=True)
+        chips = n_exp // 2
+        turn(1)
+        sum_o.relay(0)
+        for hop in range(1, chips):
+            sum_o.forward(hop)
+        turn(1)
+        red.pass_on(0)
+        turn(1)
+        for hop in range(1, chips):
+            sum_o.relay(hop)
+        turn(1)
+        sum_w.reduce()
+        sum_w.forward(0)
+        red.arrived(0)
+        gain1 = ln1_ref[0:1, :].astype(F32)
+        half = tok // 2
+        for n in range(2):
+            rows = pl.ds(n * half, half)
+            g_one = red.summed(0, n).astype(BF16).astype(F32)
+            _, xhat, inv_std = layer_norm(tok_ref[rows, :].astype(F32), gain1, 0.0)
+            gin_ref[rows, :] += norm_back(g_one, xhat, inv_std, gain1)
+            vec_own[0:1, :] += jnp.sum(g_one * xhat, axis=0, keepdims=True)
+            vec_own[1:2, :] += jnp.sum(g_one, axis=0, keepdims=True)
+        vec_seq[p.s] = vec_own[...]
+
+        def tell(other):
+            return p.to_seq(vec_own, vec_seq.at[p.s], vs_send.at[other], vs_recv.at[p.s], other)
+
+        def told(other):
+            return p.to_seq(vec_own, vec_seq.at[other], vs_send.at[other], vs_recv.at[other], other)
+
+        others = (p.near, p.far, p.diag)
+        for other in others:
+            tell(other).start()
+        turn(2)
+        for hop in range(1, chips):
+            sum_w.forward(hop)
+            sum_w.relay(hop - 1)
+            turn(1)
+        for other in others:
+            told(other).wait_recv()
+        for other in others:
+            tell(other).wait_send()
+        vec = vec_seq[0]
+        for n in range(1, n_seq):
+            vec = vec + vec_seq[n]
+        vec_own[...] = vec
+        vec_exp[p.e] = vec
+
+        def show(step):
+            other = p.peer(step, -1)
+            return p.to_exp(vec_own, vec_exp.at[p.e], ve_send.at[step], ve_recv.at[step], other)
+
+        def shown(step):
+            other = p.peer(step, 1)
+            return p.to_exp(vec_own, vec_exp.at[other], ve_send.at[step], ve_recv.at[step], other)
+
+        for step in range(1, n_exp):
+            show(step).start()
+        sum_w.relay(chips - 1)
+        turn(n_exp)
+        comb.drain()
+        out_ref[...] = (
+            resid_ref[...] + dot(pick_ref[...], ret[...].reshape(n_exp * cap, width))
+        ).astype(BF16)
+        for hop in range(chips):
+            sum_o.arrived(hop)
+        for hop in range(chips):
+            sum_w.arrived(hop)
+        for step in range(1, n_exp):
+            shown(step).wait_recv()
+            show(step).wait_send()
+        vec = vec_exp[0]
+        for n in range(1, n_exp):
+            vec = vec + vec_exp[n]
+        vec_ref[...] = vec
+        gather.drain()
+        sum_o.drain()
+        sum_w.drain()
+
+    vmem = pl.BlockSpec(memory_space=pltpu.VMEM)
+    hbm = pl.BlockSpec(memory_space=pl.ANY)
+    smem = pl.BlockSpec(memory_space=pltpu.SMEM)
+    shape = jax.ShapeDtypeStruct
+    dma = pltpu.SemaphoreType.DMA
+    return pl.pallas_call(
+        kernel,
+        out_shape=[
+            shape((tok, width), BF16),
+            shape((tok, width), F32),
+            shape((8, width), F32),
+            shape((n_seq, n_exp, rows_w, 3 * cols), BF16),
+            shape((n_seq, n_exp, rows_o, width), BF16),
+        ],
+        in_specs=[vmem] * 5 + [hbm] + [vmem] * 5 + [hbm] * 4 + [vmem, vmem, hbm, vmem, smem],
+        out_specs=[vmem, vmem, vmem, hbm, hbm],
+        scratch_shapes=[
+            pltpu.VMEM((n_seq, tok, width), BF16),
+            pltpu.VMEM((total, cols), BF16),
+            pltpu.VMEM((total, 3 * cols), BF16),
+            pltpu.VMEM((total, cols), F32),
+            pltpu.VMEM((total, cols), F32),
+            pltpu.VMEM((total, width), BF16),
+            pltpu.VMEM((width, 3 * cols), BF16),
+            pltpu.VMEM((cols, width), BF16),
+            pltpu.VMEM((n_exp, n_seq, cap, width), BF16),
+            pltpu.VMEM((1, n_seq, tok, width), BF16),
+            pltpu.VMEM((n_exp, cap, width), BF16),
+            pltpu.VMEM((8, width), F32),
+            pltpu.VMEM((n_seq, 8, width), F32),
+            pltpu.VMEM((n_exp, 8, width), F32),
+            dma((5,)),
+            dma((n_exp,)),
+            dma((n_seq,)),
+            dma((n_seq,)),
+            dma((n_exp,)),
+            dma((n_exp,)),
+        ]
+        + Gather.scratch()
+        + Combine.scratch(n_exp, cap, width)
+        + [
+            pltpu.VMEM((1, 2, tok // 2, width), BF16),
+            pltpu.VMEM((1, 4, tok // 2, width), BF16),
+            dma((1, 6)),
+            dma((1, 6)),
+        ]
+        + SumAll.scratch(n_exp, rows_o, width)
+        + SumAll.scratch(n_exp, rows_w, 3 * cols),
+        compiler_params=pltpu.CompilerParams(
+            collective_id=collective_id, has_side_effects=True, vmem_limit_bytes=VMEM_LIMIT
+        ),
+        name="back_part",
+    )(grad_back, pick, resid, ln2, cotangent, w_out, q, k, v, attn, lse, n1, *w_qkv, tokens, ln1, ffn_part,
+      b_down, lengths)
+
+
 def shards(
+    tokens, lengths, expert_ids, ln1_gain, ln1_bias, w_query, b_query, w_key, w_value, b_value, w_out, b_out,
+    ln2_gain, ln2_bias, w_up, b_up, w_down, b_down, cotangent,
+):
+    n_exp = lax.axis_size("exp")
+    n_seq = lax.axis_size("seq")
+    seq_rank = lax.axis_index("seq")
+    width = tokens.shape[2]
+    cols = width // n_seq
+    ln1 = jnp.stack([ln1_gain, ln1_bias])
+    ln2 = jnp.stack([ln2_gain, ln2_bias])
+    w_qkv = (w_query, w_key, w_value)
+    n1, q, k, v, attn, lse, resid, pick, send, cot_rows = front_part(
+        tokens[0], lengths, expert_ids[0], ln1, w_qkv, jnp.stack([b_query, b_value]), w_out, b_out[None], ln2,
+        cotangent[0], n_exp, 0,
+    )
+    grad_back, grad_w_up, grad_w_down, grad_b_up, cot_sum, ffn_part = ffn_both(
+        send, cot_rows, w_up[0], b_up, w_down[0], 1
+    )
+    grad_b_down = lax.dynamic_slice_in_dim(cot_sum, seq_rank * cols, cols, 1)
+    output, input_grad, vec, grad_qkv, grad_out = back_part(
+        grad_back, pick, resid, ln2, cotangent[0], w_out, q, k, v, attn, lse, n1, w_qkv, tokens[0], ln1, ffn_part,
+        b_down, lengths, 2,
+    )
+
+    def whole(at):
+        piece = grad_qkv[:, :, :, at * cols : (at + 1) * cols]
+        return jnp.transpose(piece, (1, 2, 0, 3)).reshape(width, width).astype(F32)
+
+    return (
+        output[None], input_grad[None], vec[0], vec[1], whole(0), vec[2], whole(1), whole(2), vec[3],
+        grad_out.reshape(width, width).astype(F32), vec[4], vec[5], vec[6],
+        grad_w_up[None], grad_b_up, grad_w_down[None], grad_b_down,
+    )
+
+
+def norm_layer(values_in, gain_vec, shift_vec):
+    center = values_in - jnp.mean(values_in, axis=-1, keepdims=True)
+    inv_std = lax.rsqrt(jnp.mean(center * center, axis=-1, keepdims=True) + EPSILON)
+    return center * inv_std * gain_vec + shift_vec
+
+
+def segment_ids(positions, seq_ends):
+    return jnp.sum((positions[:, None] >= seq_ends[None, :]).astype(jnp.int32), axis=1)
+
+
+def visible_pairs(query_pos, query_seg, key_pos, key_seg):
+    return ((query_seg[:, None] == key_seg[None, :]) & (key_pos[None, :] <= query_pos[:, None]))[
+        None
+    ]
+
+
+def project(left_op, right_op):
+    return jnp.dot(left_op, right_op, preferred_element_type=jnp.float32)
+
+
+def shards_any(
     tokens,
     lengths,
     expert_ids,
@@ -623,29 +1296,65 @@
     expert_of = expert_ids[0, :, 0]
     onehot = (expert_of[:, None] == jnp.arange(experts, dtype=jnp.int32)[None, :]).astype(jnp.int32)
     slot_of = jnp.sum(onehot * (jnp.cumsum(onehot, axis=0) - onehot), axis=1)
-    place_of = expert_of * capacity + slot_of
-    pick = (
-        place_of[:, None] == jnp.arange(experts * capacity, dtype=jnp.int32)[None, :]
-    ).astype(jnp.bfloat16)
-
-    def scatter_rows(rows):
-        laid = jnp.einsum("ts,td->sd", pick, rows, preferred_element_type=jnp.float32)
-        return laid.astype(jnp.bfloat16).reshape(experts, capacity, width)
-
-    def collect_rows(laid):
-        return project(pick, laid.reshape(experts * capacity, width))
-
-    cot_rows = dispatch_rows(scatter_rows(cotangent[0]), 0)
-    grad_back, grad_w_up, grad_w_down, grad_b_up, bias_full, ffn_part = ffn_both(
-        scatter_rows(normed_two_low), cot_rows, w_up[0], b_up, w_down[0], 1
-    )
-    returned = combine_rows(ffn_part, b_down, 2)
+    send_rows = (
+        jnp.zeros((experts, capacity, width), jnp.bfloat16)
+        .at[expert_of, slot_of]
+        .set(normed_two_low)
+    )
+    received = lax.all_to_all(send_rows, "exp", split_axis=0, concat_axis=0, tiled=True)
+    recv_count = experts * capacity
+    recv_rows = received.reshape(recv_count, width)
+    up_weight = w_up[0]
+    up_bias = b_up[0]
+    down_weight = w_down[0]
+    down_bias = b_down[0].astype(jnp.float32)
     piece_width = width // seq_size
-    grad_b_up = grad_b_up[0]
-    grad_b_down = lax.dynamic_slice_in_dim(bias_full[0], seq_rank * piece_width, piece_width, 0)
-    ffn_rows = collect_rows(returned)
+    grad_send = (
+        jnp.zeros((experts, capacity, width), jnp.bfloat16).at[expert_of, slot_of].set(cotangent[0])
+    )
+    gathered = lax.all_gather(recv_rows, "seq", axis=0, tiled=True)
+    preact = project(gathered, up_weight) + up_bias.astype(jnp.float32)
+    act_low = jax.nn.gelu(preact).astype(jnp.bfloat16)
+    part = act_low
+    expert_out = (
+        lax.psum_scatter(
+            project(part, down_weight).astype(jnp.bfloat16), "seq", scatter_dimension=0, tiled=True
+        ).astype(jnp.float32)
+        + down_bias
+    )
+    returned = lax.all_to_all(
+        expert_out.astype(jnp.bfloat16).reshape(experts, capacity, width),
+        "exp",
+        split_axis=0,
+        concat_axis=0,
+        tiled=True,
+    )
+    grad_recv = lax.all_to_all(grad_send, "exp", split_axis=0, concat_axis=0, tiled=True).reshape(
+        recv_count, width
+    )
+    grad_all = lax.all_gather(grad_recv, "seq", axis=0, tiled=True)
+    bias_full = jnp.sum(grad_all.astype(jnp.float32), axis=0)
+    grad_b_down = lax.dynamic_slice_in_dim(bias_full, seq_rank * piece_width, piece_width, 0)
+    grad_act = jnp.einsum("rd,fd->rf", grad_all, down_weight, preferred_element_type=jnp.float32)
+    grad_pre = jax.vjp(jax.nn.gelu, preact)[1](grad_act)[0].astype(jnp.bfloat16)
+    grad_w_down = jnp.einsum("rf,rd->fd", act_low, grad_all, preferred_element_type=jnp.float32)
+    grad_w_up = jnp.einsum("rd,rf->df", gathered, grad_pre, preferred_element_type=jnp.float32)
+    grad_b_up = jnp.sum(grad_pre.astype(jnp.float32), axis=0)
+    part = grad_pre
+    grad_home = lax.psum_scatter(
+        jnp.einsum("rf,df->rd", part, up_weight, preferred_element_type=jnp.float32).astype(
+            jnp.bfloat16
+        ),
+        "seq",
+        scatter_dimension=0,
+        tiled=True,
+    )
+    ffn_rows = returned[expert_of, slot_of].astype(jnp.float32)
     output = (resid + ffn_rows).astype(jnp.bfloat16)
-    grad_normed_two = collect_rows(grad_back)
+    grad_back = lax.all_to_all(
+        grad_home.reshape(experts, capacity, width), "exp", split_axis=0, concat_axis=0, tiled=True
+    )
+    grad_normed_two = grad_back[expert_of, slot_of].astype(jnp.float32)
     _, norm_two_back = jax.vjp(norm_layer, resid, gain_two, bias_two)
     grad_resid_norm, grad_gain_two, grad_bias_two = norm_two_back(grad_normed_two)
     grad_resid = cotangent[0].astype(jnp.float32) + grad_resid_norm
@@ -807,8 +1516,9 @@
         P("exp", None),
         P("exp", "seq", None),
     )
+    plane = mesh.shape["seq"] == 4 and mesh.shape["exp"] % 2 == 0
     return jax.shard_map(
-        shards,
+        shards if plane else shards_any,
         mesh=mesh,
         in_specs=placed,
         out_specs=(

time: 706 us -> 348 us (0.49)
  the two profiles are of different devices: /device:TPU:0 before, /device:TPU:25 now
where the time goes in v2:
time: 348 us; the launch traced here: 341 us
  Pallas kernels  295 us (85%)
  local copies, waits for them, and re-layouts  36.6 us (11%)
  other arithmetic  8.53 us (2%)
    pallas_call x1, Pallas kernels, back_part(): pl.pallas_call(kernel, out_shape=[shape((tok, width), BF16), shape((tok,...  131 us
    pallas_call x1, Pallas kernels, ffn_both(): pl.pallas_call(kernel, out_shape=[jax.ShapeDtypeStruct((n_exp, cap, width...  96.1 us
    pallas_call x1, Pallas kernels, front_part(): pl.pallas_call(kernel, out_shape=[shape((total, width), BF16), shape((tot...  68.1 us
    unnamed x21, local copies, waits for them, and re-layouts  26.7 us

profile of v2, /device:TPU:25, one launch (start us, length us, event | category | flops | bytes accessed | tf_op | source)
XLA Modules:
  0.0 340.9 jit_solution(8787508218443255572)
XLA Ops:
  0.7 1.5 copy.36.ids_ref
  2.1 0.7 stack.28
  2.8 0.7 stack.27
  3.5 0.7 stack.31
  4.2 0.7 stack.30
  5.5 1.3 broadcast_in_dim.15.bo_ref
  6.8 0.7 stack.34
  8.7 68.1 %front_part.1 = (bf16[1024,1024]{1,0:T(8,128)(2,1)}, bf16[1024,256]{1,0:T(8,128)(2,1)}, bf16[1024,256]{1,0:T(8,128)(2,1)}, bf16[1024,256]{1,0:T(8,128)(2,1)}, f3...) custom-call(bf16[256,1024]{1,0:T(8,128)(2,1)} %bitcast.42, ...), custom_call_target="tpu_custom_call" | custom-call | tf_op jit(solution)/shard_map/front_part/pallas_call | solution.py:650
  76.9 96.1 %ffn_both.1 = (bf16[8,64,1024]{2,1,0:T(8,128)(2,1)}, f32[1024,1024]{1,0:T(8,128)}, f32[1024,1024]{1,0:T(8,128)}, f32[1,1024]{1,0:T(1,128)}, f32[1,1024]{1,0:T(1,128)}, /*index=5*/bf16[8,4,64,1024]{3,2,1,0:T(8,128)(2,1)}) custom-call(bf16[8,64,1024]{2,1,0:T(8,128)(2,1)} %get-tuple-element.38.send, bf16[8,4,64,1024]{3,2,1,0:T(8,128)(2,1)} %get-tuple-element.39.cot_in, ...), custom_call_target="tpu_custom_call" | custom-call | tf_op jit(solution)/shard_map/ffn_both/pallas_call | solution.py:378
  173.0 130.6 %back_part.1 = (bf16[256,1024]{1,0:T(8,128)(2,1)}, f32[256,1024]{1,0:T(8,128)}, f32[8,1024]{1,0:T(8,128)}, bf16[4,8,128,768]{3,2,1,0:T(8,128)(2,1)}, bf16[4,8,32,1024]{3,2,1,0:T(8,128)(2,1)}) custom-call(bf16[8,64,1024]{2,1,0:T(8,128)(2,1)} %get-tuple-element.40.gback_ref, bf16[256,512]{1,0:T(8,128)(2,1)} %get-tuple-element.41.pick_ref, ...), custom_call_target="tpu_custom_call" | custom-call | tf_op jit(solution)/shard_map/back_part/pallas_call | solution.py:1102
  303.6 1.8 fusion
  305.4 4.7 %convert_bitcast_fusion = (f32[8,128,4,256]{3,1,0,2:T(8,128)S(1)}, f32[8,128,4,256]{3,1,0,2:T(8,128)S(1)}, f32[8,128,4,256]{3,1,0,2:T(8,128)S(1)}) fusion(bf16[4,8,128,768]{3,2,1,0:T(8,128)(2,1)} %get-tuple-element.53), kind=kLoop, calls=%fused_computation | loop fusion | flops 3145728 | bytes 18874368 | tf_op jit(solution)/shard_map/convert_element_type | solution.py:1180
  310.1 2.7 copy.43
  312.8 3.0 copy.49
  315.8 2.7 copy.44
  318.5 3.0 copy.50
  321.5 2.9 copy.45
  324.4 3.0 copy.51
  327.5 2.6 bitcast_convert_fusion
  330.1 1.2 constant_dynamic-slice_fusion
  331.4 0.8 copy.57
  332.1 1.0 copy.58
  333.1 4.9 %copy.59 = f32[1,1024,1024]{2,1,0:T(8,128)} copy(f32[1,1024,1024]{2,1,0:T(8,128)} %bitcast.38) | data formatting | bytes 8388608
  338.7 2.0 copy.61
  (14 shorter events, 2.5 us)
Async XLA Ops:
  324.4 3.1 copy-start.1
  327.5 3.9 %copy-start.3 = (bf16[256,1024]{1,0:T(8,128)(2,1)S(1)}, bf16[256,1024]{1,0:T(8,128)(2,1)}, u32[]{:S(2)}) copy-start(bf16[256,1024]{1,0:T(8,128)(2,1)} %get-tuple-element.50) | copy-start | bytes 1572868
  327.5 4.7 %copy-start.2 = (f32[256,1024]{1,0:T(8,128)S(1)}, f32[256,1024]{1,0:T(8,128)}, u32[]{:S(2)}) copy-start(f32[256,1024]{1,0:T(8,128)} %get-tuple-element.51) | copy-start | bytes 3145732
  333.1 4.9 %copy-start.4 = (f32[1,1024]{1,0:T(1,128)S(1)}, f32[1,1024]{1,0:T(1,128)}, u32[]{:S(2)}) copy-start(f32[1,1024]{1,0:T(1,128)} %get-tuple-element.119) | copy-start | bytes 12292
  333.1 5.5 %copy-start = (f32[1024,1024]{1,0:T(8,128)S(1)}, f32[1024,1024]{1,0:T(8,128)}, u32[]{:S(2)}) copy-start(f32[1024,1024]{1,0:T(8,128)} %get-tuple-element.57) | copy-start | bytes 12582916
